TPU v7x, 128 devices: a whole 4x4x4 slice. The times are simulated.
128 devices in a mesh: gx: 8 (over z, core), gy: 16 (over y, x).
Axes of the slice: x: 4, y: 4, z: 4, core: 2. Of those that a mesh axis runs over, the one named last changes fastest.
Arguments:
- charges: float32 [8192, 128], P(('gx', 'gy')), may hold values from -0.8 to 0.8
- positions: float32 [8192, 3, 128], P(('gx', 'gy')), may hold values from 0 to 1
- widths: float32 [8192, 128], P(('gx', 'gy')), may hold values from 0.05 to 0.5
- site_counts: int32 [8192], P(('gx', 'gy')), may hold values from 1 to 128, 786432 in all
- pair_records: int32 [32768, 3], P(('gx', 'gy')), may hold values from 0 to 127, as said below
Outputs:
- near_potential: float32 [8192, 128], P(('gx', 'gy'))
- far_potential: float32 [8192], P(('gx', 'gy'))
Inputs may be any that keep to these rules, and one draw needn't show every extreme that they name: `pair_records`: rows k * 256 to (k + 1) * 256 - 1 are the pairs owned by device k. Each row names a home device and two different local boxes of that device's 4 x 4 x 4 block whose cells touch (differ by at most 1 in every coordinate). Among one owner's rows at most 8 name one home device, and some home device is named exactly 8 times by every owner.
All inputs are finite; a program needn't handle non-finite values. No bound on the sum of `site_counts` on one device may be relied on, other than what follows from the above.
Results may differ from a plain program's by a relative error of at most 0.0003.
Values sent between devices are 32-bit elements; how exact they have to be, the bound alone decides.
A program may use at most 64 MiB of HBM per device.

v0:
```python
import jax
import jax.numpy as jnp
from jax import lax
from jax.sharding import PartitionSpec as P

CAP = 8


SOFT_TERM = 2.0


def box_coords(box_index):
    return jnp.stack([box_index // 16, box_index // 4 % 4, box_index % 4], axis=-1).astype(
        jnp.float32
    )


def parent_local(local_box):
    return local_box // 32 * 4 + local_box // 8 % 2 * 2 + local_box % 4 // 2


def pair_terms(block_first, block_second, box_first, box_second):
    offset_box = box_coords(box_second) - box_coords(box_first)
    sites = block_first.shape[2]
    distance = jnp.zeros((block_first.shape[0], sites, sites), jnp.float32)
    for axis_number in range(3):
        delta_axis = (
            offset_box[:, axis_number, None, None]
            + block_second[:, 1 + axis_number, None, :]
            - block_first[:, 1 + axis_number, :, None]
        )
        distance = distance + delta_axis * delta_axis
    pair_width = block_first[:, 4, :, None] + block_second[:, 4, None, :]
    kernel = lax.rsqrt(distance + pair_width) - lax.rsqrt(distance + pair_width + SOFT_TERM)
    phi_first = jnp.einsum(
        "nij,nj->ni", kernel, block_second[:, 0], precision=lax.Precision.HIGHEST
    )
    phi_second = jnp.einsum(
        "nij,ni->nj", kernel, block_first[:, 0], precision=lax.Precision.HIGHEST
    )
    return (phi_first, phi_second)


def far_field(parent_charge, device_flat, local_box, count_gy):
    box_xyz = (
        jnp.stack(
            [
                4 * (device_flat // count_gy) + local_box // 16,
                4 * (device_flat % count_gy) + local_box // 4 % 4,
                local_box % 4,
            ],
            axis=-1,
        ).astype(jnp.float32)
        + 0.5
    )
    parent_all = jnp.arange(parent_charge.shape[0])
    parent_dev = parent_all // 8
    parent_own = parent_all % 8
    parent_xyz = (
        jnp.stack(
            [
                4 * (parent_dev // count_gy) + 2 * (parent_own // 4),
                4 * (parent_dev % count_gy) + 2 * (parent_own // 2 % 2),
                2 * (parent_own % 2),
            ],
            axis=-1,
        ).astype(jnp.float32)
        + 1.0
    )
    distance = jnp.zeros((box_xyz.shape[0], parent_xyz.shape[0]), jnp.float32)
    for axis_number in range(3):
        delta_axis = box_xyz[:, axis_number, None] - parent_xyz[None, :, axis_number]
        distance = distance + delta_axis * delta_axis
    return jnp.sum(lax.rsqrt(distance + SOFT_TERM) * parent_charge[None, :], axis=1)


def spread_sum(target_ids, values_flat, box_total):
    onehot = (jnp.arange(box_total)[:, None] == target_ids[None, :]).astype(jnp.float32)
    return jnp.dot(onehot, values_flat, precision=lax.Precision.HIGHEST)


def body(charges, positions, widths, site_counts, pair_records):
    count_gx = lax.axis_size("gx")
    count_gy = lax.axis_size("gy")
    count_dev = count_gx * count_gy
    box_total, sites = charges.shape
    site_live = lax.broadcasted_iota(jnp.int32, (box_total, sites), 1) < site_counts[:, None]
    charge_live = jnp.where(site_live, charges, jnp.float32(0.0))
    box_block = jnp.concatenate([charge_live[:, None, :], positions, widths[:, None, :]], axis=1)
    local_box = jnp.arange(box_total)
    parent_map = (jnp.arange(8)[:, None] == parent_local(local_box)[None, :]).astype(jnp.float32)
    parent_mine = jnp.dot(parent_map, jnp.sum(charge_live, axis=1), precision=lax.Precision.HIGHEST)
    parent_charge = lax.all_gather(parent_mine, ("gx", "gy"), axis=0, tiled=True)
    device_flat = lax.axis_index("gx") * count_gy + lax.axis_index("gy")
    far_potential = far_field(parent_charge, device_flat, local_box, count_gy)
    home_dev = pair_records[:, 0]
    box_first = pair_records[:, 1]
    box_second = pair_records[:, 2]
    rows_own = pair_records.shape[0]
    same_home = home_dev[:, None] == home_dev[None, :]
    earlier = lax.broadcasted_iota(jnp.int32, (rows_own, rows_own), 0) > lax.broadcasted_iota(
        jnp.int32, (rows_own, rows_own), 1
    )
    rank_within = jnp.sum((same_home & earlier).astype(jnp.int32), axis=1)
    slot_index = home_dev * CAP + rank_within
    entries = jnp.stack([box_first, box_second, jnp.ones_like(box_first)], axis=1)
    requests = jnp.zeros((count_dev * CAP, 3), jnp.int32).at[slot_index].set(entries)
    asked_part = lax.all_to_all(
        requests.reshape(count_dev, CAP, 3), ("gx", "gy"), split_axis=0, concat_axis=0, tiled=True
    )
    packed = box_block[asked_part[..., 0:2]]
    fetched = lax.all_to_all(packed, ("gx", "gy"), split_axis=0, concat_axis=0, tiled=True)
    fetched = fetched.reshape(count_dev * CAP, 2, 5, sites)
    mine = fetched[slot_index]
    phi_first, phi_second = pair_terms(mine[:, 0], mine[:, 1], box_first, box_second)
    outgoing = (
        jnp.zeros((count_dev * CAP, 2, sites), jnp.float32)
        .at[slot_index]
        .set(jnp.stack([phi_first, phi_second], axis=1))
    )
    returned = lax.all_to_all(
        outgoing.reshape(count_dev, CAP, 2, sites),
        ("gx", "gy"),
        split_axis=0,
        concat_axis=0,
        tiled=True,
    )
    target_ids = asked_part[..., 0:2].reshape(-1)
    near = spread_sum(target_ids, returned.reshape(-1, sites), box_total)
    near_potential = jnp.where(site_live, near, jnp.float32(0.0))
    return (near_potential, far_potential)


def solution(mesh):
    return jax.shard_map(
        body,
        mesh=mesh,
        in_specs=(
            P(("gx", "gy"), None),
            P(("gx", "gy"), None, None),
            P(("gx", "gy"), None),
            P(("gx", "gy")),
            P(("gx", "gy"), None),
        ),
        out_specs=(P(("gx", "gy"), None), P(("gx", "gy"))),
        check_vma=False,
    )
```

profile of v0, /device:TPU:1, one launch (start us, length us, event | category | flops | bytes accessed | tf_op | source)
XLA Modules:
  0.0 335.2 jit_solution(17073304791224933422)
XLA Ops:
  0.6 0.7 slice.79
  1.3 0.7 slice.80
  2.0 0.2 convert_reduce_fusion
  2.2 0.8 and_select_fusion.9
  3.0 0.1 copy.40
  3.2 1.3 scatter_custom_fusion
  4.5 1.5 copy.27
  6.0 11.5 %all-to-all-start = ((s32[128,8,3]{1,2,0:T(4,128)}), s32[128,8,3]{1,2,0:T(4,128)S(1)}, u32[]{:S(2)}, u32[]{:S(2)}) async-start(s32[128,8,3]{1,2,0:T(4,128)} %copy.27), calls=%async_computation | async-start | bytes 524288 | tf_op jit(solution)/shard_map/all_to_all | solution.py:108
  17.5 1.0 copy.30
  18.5 0.9 fusion.53
  19.4 0.9 pad_maximum_fusion
  20.3 8.5 %all-to-all-done = s32[128,8,3]{1,2,0:T(4,128)S(1)} async-done(((s32[128,8,3]{1,2,0:T(4,128)}), s32[128,8,3]{1,2,0:T(4,128)S(1)}, u32[]{:S(2)}, u32[]{:S(2)}) %all-to-all-start) | async-done | bytes 12320 | tf_op jit(solution)/shard_map/all_to_all | solution.py:108
  28.8 0.1 fusion.57
  28.8 0.8 copy.31
  29.7 0.3 reshape.478
  29.9 17.6 %gather_fusion = f32[2048,5,128]{2,1,0:T(8,128)} fusion(f32[64,5,128]{2,1,0:T(8,128)S(1)} %pad_maximum_fusion, s32[2048]{0:T(1024)S(1)} %broadcast_clamp_fusion), kind=kCustom, calls=%fused_computation | custom fusion | bytes 10493952 | tf_op jit(solution)/shard_map/gather | solution.py:111
  47.5 8.3 %copy.32 = f32[128,8,2,5,128]{4,1,3,2,0:T(8,128)} copy(f32[128,8,2,5,128]{4,3,2,1,0:T(8,128)} %bitcast.66) | data formatting | bytes 10485760 | tf_op jit(solution)/shard_map/gather | solution.py:111
  55.9 5.2 %all-to-all-start.1 = ((f32[128,8,2,5,128]{4,1,3,2,0:T(8,128)}), f32[128,8,2,5,128]{4,1,3,2,0:T(8,128)}, u32[]{:S(2)}, u32[]{:S(2)}) async-start(f32[128,8,2,5,128]{4,1,3,2,0:T(8,128)} %copy.32), calls=%async_computation.1 | async-start | bytes 10485760 | tf_op jit(solution)/shard_map/all_to_all | solution.py:112
  61.2 0.1 convolution_bitcast_fusion
  61.3 62.7 %all-to-all-done.1 = f32[128,8,2,5,128]{4,1,3,2,0:T(8,128)} async-done(((f32[128,8,2,5,128]{4,1,3,2,0:T(8,128)}), f32[128,8,2,5,128]{4,1,3,2,0:T(8,128)}, u32[]{:S(2)}, u32[]{:S(2)}) %all-to-all-start.1) | async-done | bytes 5242912 | tf_op jit(solution)/shard_map/all_to_all | solution.py:112
  124.0 7.5 %copy.33 = f32[128,8,2,5,128]{4,2,3,1,0:T(2,128)} copy(f32[128,8,2,5,128]{4,1,3,2,0:T(8,128)} %all-to-all-done.1) | data formatting | bytes 10485760 | tf_op jit(solution)/shard_map/all_to_all | solution.py:112
  131.6 4.6 %gather_fusion.1 = f32[256,2,5,128]{3,1,2,0:T(2,128)S(1)} fusion(f32[1024,2,5,128]{3,1,2,0:T(2,128)} %bitcast.67, s32[1024]{0:T(1024)S(1)} %pad_clamp_fusion), kind=kCustom, calls=%fused_computation.1 | custom fusion | bytes 2622464 | tf_op jit(solution)/shard_map/gather | solution.py:114
  136.2 1.0 fusion.55
  137.2 0.1 copy_bitcast_fusion
  137.3 0.2 fusion.56
  137.5 51.8 %fusion.1 = f32[256,1,128]{2,1,0:T(1,128)S(1)} fusion(f32[256,128,1]{1,2,0:T(1,128)S(1)} %bitcast.72, f32[256,128]{1,0:T(8,128)S(1)} %get-tuple-element.11, f32[256,128]{1,0:T(8,128)S(1)} %get-tuple-element.17, f32[256,128]{1,0:T(8,128)S(1)} %get-tuple-element.18, f32[256,128]{1,0:T(8,128)S(1)} %get-tuple-element.12, f32[256,128]{1,0:T(8,128)S(1)} %get-tuple-element.19, ...), kind=kOutput, calls=%fused_computation.6 | convolution fusion | flops 100663296 | bytes 1310720 | tf_op jit(solution)/shard_map/nij,nj->ni/dot_general | solution.py:35
  189.3 0.0 copy-start
  189.3 40.9 %fusion = f32[256,1,128]{2,1,0:T(1,128)S(1)} fusion(f32[256,128,1]{1,2,0:T(1,128)S(1)} %bitcast.71, f32[256,128]{1,0:T(8,128)S(1)} %get-tuple-element.11, f32[256,128]{1,0:T(8,128)S(1)} %get-tuple-element.17, f32[256,128]{1,0:T(8,128)S(1)} %get-tuple-element.18, f32[256,128]{1,0:T(8,128)S(1)} %get-tuple-element.12, f32[256,128]{1,0:T(8,128)S(1)} %get-tuple-element.19, ...), kind=kOutput, calls=%fused_computation.5 | convolution fusion | flops 100663296 | bytes 1310720 | tf_op jit(solution)/shard_map/nij,ni->nj/dot_general | solution.py:38
  230.2 0.2 pad_maximum_fusion.1
  230.5 1.2 broadcast_in_dim.29
  231.7 24.2 %scatter_fusion = f32[1024,2,128]{2,1,0:T(2,128)} fusion(f32[1024,2,128]{2,1,0:T(2,128)} %broadcast_in_dim.29, s32[256]{0:T(256)S(1)} %bitcast.76, f32[256,2,128]{2,1,0:T(2,128)S(1)} %pad_maximum_fusion.1), kind=kCustom, calls=%fused_computation.3 | custom fusion | bytes 787456 | tf_op jit(solution)/shard_map/scatter | solution.py:119
  255.9 5.7 %all-to-all-start.2 = ((f32[128,8,2,128]{3,2,1,0:T(2,128)}), f32[128,8,2,128]{3,2,1,0:T(2,128)S(1)}, u32[]{:S(2)}, u32[]{:S(2)}) async-start(f32[128,8,2,128]{3,2,1,0:T(2,128)} %bitcast.32), calls=%async_computation.2 | async-start | bytes 2097152 | tf_op jit(solution)/shard_map/all_to_all | solution.py:121
  261.6 0.2 dynamic-update-slice
  261.9 70.2 %all-reduce.1 = f32[1024]{0:T(1024)S(1)} all-reduce(f32[1024]{0:T(1024)S(1)} %dynamic-update-slice), channel_id=1, replica_groups=mesh['gx'=8,'gy'=16] {'gx','gy'}, use_global_device_ids=true, to_apply=%add.1 | all-reduce | flops 1024 | bytes 8192
  332.2 0.8 multiply_reduce_fusion
  333.0 0.8 copy.28
  333.8 0.3 eq.65
  334.0 0.0 all-to-all-done.2
  334.1 0.0 copy-done
  334.1 1.2 convolution_select_fusion
  (15 shorter events, 0.2 us)
Async XLA Ops:
  6.0 22.8 %all-to-all-start = ((s32[128,8,3]{1,2,0:T(4,128)}), s32[128,8,3]{1,2,0:T(4,128)S(1)}, u32[]{:S(2)}, u32[]{:S(2)}) async-start(s32[128,8,3]{1,2,0:T(4,128)} %copy.27), calls=%async_computation | async-start | bytes 524288 | tf_op jit(solution)/shard_map/all_to_all | solution.py:108
  55.9 68.2 %all-to-all-start.1 = ((f32[128,8,2,5,128]{4,1,3,2,0:T(8,128)}), f32[128,8,2,5,128]{4,1,3,2,0:T(8,128)}, u32[]{:S(2)}, u32[]{:S(2)}) async-start(f32[128,8,2,5,128]{4,1,3,2,0:T(8,128)} %copy.32), calls=%async_computation.1 | async-start | bytes 10485760 | tf_op jit(solution)/shard_map/all_to_all | solution.py:112
  189.3 144.8 %copy-start = (s32[64]{0:T(128)S(1)}, s32[64]{0:T(128)}, u32[]{:S(2)}) copy-start(s32[64]{0:T(128)} %param.8) | copy-start | bytes 772
  255.9 78.2 %all-to-all-start.2 = ((f32[128,8,2,128]{3,2,1,0:T(2,128)}), f32[128,8,2,128]{3,2,1,0:T(2,128)S(1)}, u32[]{:S(2)}, u32[]{:S(2)}) async-start(f32[128,8,2,128]{3,2,1,0:T(2,128)} %bitcast.32), calls=%async_computation.2 | async-start | bytes 2097152 | tf_op jit(solution)/shard_map/all_to_all | solution.py:121
where the time goes:
time: 336 us; the launch traced here: 335 us
  matrix products  94 us (28%)
  local copies, waits for them, and re-layouts  72.3 us (22%)
  waiting for transfers between devices  71.2 us (21%)
  blocking collectives  70.2 us (21%)
  starting transfers between devices  22.4 us (7%)
  other arithmetic  4.28 us (1%)
    unnamed x1, blocking collectives  70.2 us
    all_to_all x1, waiting for transfers between devices, body(): lax.all_to_all(packed, ('gx', 'gy'), split_axis=0, concat_axis=0, tiled=T...  62.7 us
    dot_general x1, matrix products, pair_terms(): jnp.einsum('nij,nj->ni', kernel, block_second[:, 0], precision=lax.Precis...  51.8 us
    dot_general x1, matrix products, pair_terms(): jnp.einsum('nij,ni->nj', kernel, block_first[:, 0], precision=lax.Precisi...  40.9 us
    gather x2, local copies, waits for them, and re-layouts, body(): packed = box_block[asked_part[..., 0:2]]  25.9 us
    scatter x1, local copies, waits for them, and re-layouts, body(): outgoing = jnp.zeros((count_dev * CAP, 2, sites), jnp.float32).at[slot_in...  24.2 us
    all_to_all x1, starting transfers between devices, body(): lax.all_to_all(requests.reshape(count_dev, CAP, 3), ('gx', 'gy'), split_a...  11.5 us
    all_to_all x1, waiting for transfers between devices, body(): lax.all_to_all(requests.reshape(count_dev, CAP, 3), ('gx', 'gy'), split_a...  8.5 us
  transfers between devices with their start and end apart: 3, of which 2 were waited for; matrix products, arithmetic and copies ran while one was open for 2% of the time, Pallas kernels for 0%

commit v1 on v0

v1 whole, which is shorter than its diff:
```python
import jax
import jax.numpy as jnp
from jax import lax
from jax.experimental import pallas as pl
from jax.experimental.pallas import tpu as pltpu
from jax.sharding import PartitionSpec as P

F32, BF16, I32 = jnp.float32, jnp.bfloat16, jnp.int32
MESH = pl.DeviceIdType.MESH
GX, GY, CAP = 8, 16, 8
DEVICES = GX * GY
DEPTH = 48
SOFT_TERM = 2.0


def iota(shape, dim):
    return lax.broadcasted_iota(I32, shape, dim)


def dot(a, b):
    return jnp.dot(a, b, preferred_element_type=F32)


def dot_nt(a, b):
    return lax.dot_general(a, b, (((1,), (1,)), ((), ())), preferred_element_type=F32)


def span(ka):
    return max(ka - 1, 0), min(ka + 1, 3)


def rows(start, size):
    return pl.ds(pl.multiple_of(start, size), size)


def split3(x):
    h = x.astype(BF16).astype(F32)
    r = x - h
    m = r.astype(BF16).astype(F32)
    return h, m, r - m


def column(row):
    eye = iota((64, 64), 0) == iota((64, 64), 1)
    return jnp.sum(jnp.where(eye, row, 0.0), axis=1, keepdims=True)


def messages(rec_ref, ql_ref, send_ref):
    home, first, second = rec_ref[0:1], rec_ref[1:2], rec_ref[2:3]
    named = jnp.where(iota((DEVICES, 256), 0) == home, 1.0, 0.0)
    earlier = jnp.where(iota((256, 256), 0) < iota((256, 256), 1), 1.0, 0.0).astype(BF16)
    before = dot(named.astype(BF16), earlier)
    rank = jnp.sum(named * before, axis=0, keepdims=True).astype(I32)
    slot = iota((DEVICES, 256), 0)
    values = jnp.where(slot == rank, first + 1, jnp.where(slot == rank + CAP, second + 1, 0))
    out = dot_nt(named.astype(BF16), values.astype(F32).astype(BF16))
    box = iota((64, 128), 0)
    parent = box // 32 * 4 + box // 8 % 2 * 2 + box % 4 // 2
    charge = jnp.sum(ql_ref[...], axis=1, keepdims=True)
    mine = jnp.where(iota((64, 128), 1) == parent + 2 * CAP, charge, 0.0)
    send_ref[...] = out + jnp.sum(mine, axis=0, keepdims=True)


def planes(pos_ref, wid_ref, left_ref, right_ref):
    box = iota((64, 128), 0)
    cells = (box // 16, box // 4 % 4, box % 4)
    norm = wid_ref[...]
    one, zero = jnp.ones((64, 128), F32), jnp.zeros((64, 128), F32)
    for c in range(3):
        x = pos_ref[c] + (cells[c].astype(F32) - 2.0)
        norm = norm + x * x
        left_ref[c] = -2.0 * x
        right_ref[c] = x
    left_ref[3], right_ref[3] = norm, one
    left_ref[4], right_ref[4] = one, norm
    for c in range(5, 8):
        left_ref[c] = zero
        right_ref[c] = zero


def features(r, left_ref, right_ref, ql_ref, lt_ref, rt_ref, qc_ref):
    eye = jnp.where(iota((128, 128), 0) == iota((128, 128), 1), 1.0, 0.0).astype(BF16)
    pad = jnp.zeros((128 - DEPTH, 128), BF16)
    packed = []
    for k in range(4):
        b = 4 * r + k
        h, m, l = split3(left_ref[:, b, :])
        packed.append(jnp.concatenate([h, h, m, m, h, l], axis=0).astype(BF16))
        h, m, l = split3(right_ref[:, b, :])
        rt_ref[r, :, 128 * k : 128 * k + 128] = jnp.concatenate([h, m, h, m, l, h], axis=0).astype(BF16)
    for k in (0, 2):
        t = dot_nt(eye, jnp.concatenate([packed[k], pad, packed[k + 1], pad], axis=0))
        for kk in (0, 1):
            lt_ref[rows((4 * r + k + kk) * 128, 128), :] = t[:, 128 * kk : 128 * kk + DEPTH].astype(BF16)
    for k in range(4):
        b = 4 * r + k
        h, m, l = split3(jnp.broadcast_to(ql_ref[pl.ds(b, 1), :], (128, 128)))
        t = dot_nt(eye, h.astype(BF16)) + dot_nt(eye, m.astype(BF16)) + dot_nt(eye, l.astype(BF16))
        qc_ref[rows(b * 128, 128), :] = t


def kernel_block(r1, ka, r2, lo, hi, lt_ref, rt_ref):
    left = lt_ref[rows(r1 * 512 + ka * 128, 128), :]
    d = dot(left, rt_ref[r2, :, lo * 128 : (hi + 1) * 128])
    return lax.rsqrt(d) - lax.rsqrt(d + SOFT_TERM)


def produce(r1, r2, slot, lt_ref, rt_ref, k_ref):
    for ka in range(4):
        lo, hi = span(ka)
        k_ref[slot, ka, :, lo * 128 : (hi + 1) * 128] = kernel_block(r1, ka, r2, lo, hi, lt_ref, rt_ref)


def consume(r1, r2, block, spans, ql_ref, qc_ref, cnt_ref, acc1_ref, acc2_ref, diff):
    crow = cnt_ref[pl.ds(r1, 1), :]
    back = {}
    for ka, (lo, hi) in spans:
        k = block(ka)
        qc = qc_ref[rows(r1 * 512 + ka * 128, 128), :].reshape(16, 8, 128)
        total = None
        for kb in range(lo, hi + 1):
            lane = diff * 16 + 4 * ka + kb
            c = jnp.broadcast_to(crow[:, lane : lane + 1], (8, 128))
            kk = k[:, (kb - lo) * 128 : (kb - lo + 1) * 128].reshape(16, 8, 128)
            cq = c * jnp.broadcast_to(ql_ref[pl.ds(4 * r2 + kb, 1), :], (8, 128))
            part = kk * cq[None]
            total = part if total is None else total + part
            b = jnp.sum(kk * qc, axis=0) * c
            back[kb] = b if kb not in back else back[kb] + b
        acc1_ref[4 * r1 + ka] += total.reshape(128, 128)
    for kb, b in back.items():
        acc2_ref[4 * r2 + kb] += b


CROSS = [(ka, span(ka)) for ka in range(4)]
OWN = [(ka, (ka + 1, ka + 1)) for ka in range(3)]


def count_pairs(got, cnt_ref):
    c = jnp.zeros((16, 128), F32)
    for k in range(CAP):
        a, b = got[k : k + 1].astype(I32) - 1, got[CAP + k : CAP + 1 + k].astype(I32) - 1
        first, second = jnp.minimum(a, b), jnp.maximum(a, b)
        r1, r2 = first // 4, second // 4
        lane = (r2 - r1) * 16 + first % 4 * 4 + second % 4
        hot1 = jnp.where(iota((16, 128), 0) == r1, 1.0, 0.0).astype(BF16)
        hot2 = jnp.where((iota((128, 128), 0) == lane) & (first >= 0), 1.0, 0.0).astype(BF16)
        c = c + dot_nt(hot1, hot2)
    cnt_ref[...] = c


def far_field(got, u, v):
    g, src = iota((64, 128), 0), iota((64, 128), 1)
    dx0 = (4 * (u - src % GX) + g // 16).astype(F32) + 0.5
    dy0 = (4 * (v - src // GX) + g // 4 % 4).astype(F32) + 0.5
    dz0 = (g % 4).astype(F32) + 0.5
    total = jnp.zeros((64, 128), F32)
    for p in range(8):
        dx = dx0 - (2 * (p // 4) + 1)
        dy = dy0 - (2 * (p // 2 % 2) + 1)
        dz = dz0 - (2 * (p % 2) + 1)
        total = total + lax.rsqrt(dx * dx + dy * dy + dz * dz + SOFT_TERM) * got[2 * CAP + p : 2 * CAP + 1 + p]
    col = jnp.sum(total, axis=1, keepdims=True)
    eye = iota((64, 64), 0) == iota((64, 64), 1)
    return jnp.sum(jnp.where(eye, col, 0.0), axis=0, keepdims=True)


def collect(acc1_ref, acc2_ref, live, out_ref):
    row = iota((16, 128), 0)

    def step(g, carry):
        total = jnp.zeros((16, 128), F32)
        for k in range(8):
            b = 8 * g + k
            x = acc1_ref[b]
            h = x.astype(BF16)
            low = (x - h.astype(F32)).astype(BF16)
            pick = jnp.where(row == k, 1.0, 0.0).astype(BF16)
            total = total + dot_nt(pick, h) + dot_nt(pick, low)
            s = jnp.sum(acc2_ref[b], axis=0, keepdims=True)
            total = total + jnp.where(row == k, s, 0.0)
        out_ref[rows(8 * g, 8), :] = total[:8]
        return carry

    lax.fori_loop(0, 8, step, 0)
    out_ref[...] = jnp.where(live, out_ref[...], 0.0)


def kernel(
    q_ref, pos_ref, wid_ref, cnt_ref, rec_ref, near_ref, far_ref,
    left_ref, right_ref, lt_ref, rt_ref, ql_ref, qc_ref, k_ref, c_ref, acc1_ref, acc2_ref,
    send_ref, mid_ref, turn_ref, got_ref, send1, recv1, send2, recv2,
):
    u, v = lax.axis_index("gx"), lax.axis_index("gy")
    others_x = [lax.rem(u + s, GX) for s in range(1, GX)]
    others_y = [lax.rem(v + s, GY) for s in range(1, GY)]
    barrier = pltpu.get_barrier_semaphore()
    for x in others_x:
        pl.semaphore_signal(barrier, inc=1, device_id=(x, v), device_id_type=MESH)
    for y in others_y:
        pl.semaphore_signal(barrier, inc=1, device_id=(u, y), device_id_type=MESH)

    cnt = column(cnt_ref[...].astype(F32)).astype(I32)
    live = iota((64, 128), 1) < cnt
    ql_ref[...] = jnp.where(live, q_ref[...], 0.0)
    messages(rec_ref, ql_ref, send_ref)
    pl.semaphore_wait(barrier, GX + GY - 2)

    first = [
        pltpu.make_async_remote_copy(
            src_ref=send_ref.at[rows(x * GY, GY)],
            dst_ref=mid_ref.at[rows(u * GY, GY)],
            send_sem=send1.at[s],
            recv_sem=recv1.at[s],
            device_id=(x, v),
            device_id_type=MESH,
        )
        for s, x in enumerate(others_x)
    ]
    for copy in first:
        copy.start()
    mid_ref[rows(u * GY, GY), :] = send_ref[rows(u * GY, GY), :]

    acc1_ref[...] = jnp.zeros_like(acc1_ref)
    acc2_ref[...] = jnp.zeros_like(acc2_ref)
    planes(pos_ref, wid_ref, left_ref, right_ref)

    def feature_step(r, carry):
        features(r, left_ref, right_ref, ql_ref, lt_ref, rt_ref, qc_ref)
        return carry

    lax.fori_loop(0, 16, feature_step, 0)

    for copy in first:
        copy.wait_recv()
    for y in range(GY):
        turn_ref[y * GX : (y + 1) * GX, :] = mid_ref[pl.ds(y, GX, stride=GY), :]
    second = [
        pltpu.make_async_remote_copy(
            src_ref=turn_ref.at[rows(y * GX, GX)],
            dst_ref=got_ref.at[rows(v * GX, GX)],
            send_sem=send2.at[s],
            recv_sem=recv2.at[s],
            device_id=(u, y),
            device_id_type=MESH,
        )
        for s, y in enumerate(others_y)
    ]
    for copy in second:
        copy.start()
    got_ref[rows(v * GX, GX), :] = turn_ref[rows(v * GX, GX), :]

    def produce_step(i, carry):
        for j in range(3):
            produce(4 * i + j, 4 * i + j + 1, 3 * i + j, lt_ref, rt_ref, k_ref)
        return carry

    lax.fori_loop(0, 4, produce_step, 0)

    for copy in second:
        copy.wait_recv()
    got = got_ref[...].T
    count_pairs(got, c_ref)
    far_ref[...] = far_field(got, u, v)

    sums = (ql_ref, qc_ref, c_ref, acc1_ref, acc2_ref)

    def direct(r1, diff, spans):
        r2, of = r1 + diff, dict(spans)
        consume(r1, r2, lambda ka: kernel_block(r1, ka, r2, *of[ka], lt_ref, rt_ref), spans, *sums, diff)

    for dj in (-1, 1):

        def diagonal_step(i, carry, dj=dj):
            for j in range(3):
                direct(4 * i + j + (dj < 0), 4 + dj, CROSS)
            return carry

        lax.fori_loop(0, 3, diagonal_step, 0)

    def straight_step(i, carry):
        for j in range(4):
            p = 4 * i + j
            direct(p, 4, CROSS)

            def block(ka, p=p):
                lo, hi = span(ka)
                return k_ref[p, ka, :, lo * 128 : (hi + 1) * 128]

            r1 = p // 3 * 4 + p % 3
            consume(r1, r1 + 1, block, CROSS, *sums, 1)
        return carry

    lax.fori_loop(0, 3, straight_step, 0)

    def own_step(i, carry):
        for j in range(4):
            direct(4 * i + j, 0, OWN)
        return carry

    lax.fori_loop(0, 4, own_step, 0)

    collect(acc1_ref, acc2_ref, live, near_ref)
    for copy in first + second:
        copy.wait_send()


def body(charges, positions, widths, site_counts, pair_records):
    vmem = pltpu.VMEM
    near, far = pl.pallas_call(
        kernel,
        out_shape=(jax.ShapeDtypeStruct((64, 128), F32), jax.ShapeDtypeStruct((1, 64), F32)),
        in_specs=[pl.BlockSpec(memory_space=vmem)] * 5,
        out_specs=(pl.BlockSpec(memory_space=vmem),) * 2,
        scratch_shapes=[
            vmem((8, 64, 128), F32),
            vmem((8, 64, 128), F32),
            vmem((8192, DEPTH), BF16),
            vmem((16, DEPTH, 512), BF16),
            vmem((64, 128), F32),
            vmem((8192, 128), F32),
            vmem((12, 4, 128, 512), F32),
            vmem((16, 128), F32),
            vmem((64, 128, 128), F32),
            vmem((64, 8, 128), F32),
            vmem((DEVICES, 128), F32),
            vmem((DEVICES, 128), F32),
            vmem((DEVICES, 128), F32),
            vmem((DEVICES, 128), F32),
            pltpu.SemaphoreType.DMA((GX - 1,)),
            pltpu.SemaphoreType.DMA((GX - 1,)),
            pltpu.SemaphoreType.DMA((GY - 1,)),
            pltpu.SemaphoreType.DMA((GY - 1,)),
        ],
        compiler_params=pltpu.CompilerParams(collective_id=0, has_side_effects=True, vmem_limit_bytes=56 << 20),
    )(charges, positions.transpose(1, 0, 2), widths, site_counts.reshape(1, 64), pair_records.T)
    return near, far.reshape(64)


def solution(mesh):
    return jax.shard_map(
        body,
        mesh=mesh,
        in_specs=(
            P(("gx", "gy"), None),
            P(("gx", "gy"), None, None),
            P(("gx", "gy"), None),
            P(("gx", "gy")),
            P(("gx", "gy"), None),
        ),
        out_specs=(P(("gx", "gy"), None), P(("gx", "gy"))),
        check_vma=False,
    )
```

time: 336 us -> 39.9 us (0.12)
  matrix products: 94 us -> 0 us
  waiting for transfers between devices: 71.2 us -> 0 us
  local copies, waits for them, and re-layouts: 72.3 us -> 1.89 us
  blocking collectives: 70.2 us -> 0 us
  Pallas kernels: 0 us -> 37.1 us
  starting transfers between devices: 22.4 us -> 0 us
  other arithmetic: 4.28 us -> 0 us
    dot_general x4 -> x0, matrix products: 94 us -> none  [the longest x1 51.8 us: pair_terms(): jnp.einsum('nij,nj->ni', kernel, block_second[:, 0], precision=lax.Precis...]
    all_to_all x3 -> x0, waiting for transfers between devices: 71.2 us -> none  [the longest x1 62.7 us: body(): lax.all_to_all(packed, ('gx', 'gy'), split_axis=0, concat_axis=0, tiled=T...]
    unnamed x1 -> x0, blocking collectives: 70.2 us -> none
    pallas_call x0 -> x1, Pallas kernels: none -> 37.1 us  [body(): pl.pallas_call(kernel, out_shape=(jax.ShapeDtypeStruct((64, 128), F32), j...]
    gather x3 -> x0, local copies, waits for them, and re-layouts: 30.5 us -> none  [the longest x2 25.9 us: body(): packed = box_block[asked_part[..., 0:2]]]
    scatter x2 -> x0, local copies, waits for them, and re-layouts: 25.5 us -> none  [the longest x1 24.2 us: body(): outgoing = jnp.zeros((count_dev * CAP, 2, sites), jnp.float32).at[slot_in...]
    all_to_all x3 -> x0, starting transfers between devices: 22.4 us -> none  [the longest x1 11.5 us: body(): lax.all_to_all(requests.reshape(count_dev, CAP, 3), ('gx', 'gy'), split_a...]
    all_to_all x1 -> x0, local copies, waits for them, and re-layouts: 7.5 us -> none  [body(): lax.all_to_all(packed, ('gx', 'gy'), split_axis=0, concat_axis=0, tiled=T...]
  transfers between devices with their start and end apart: 3 -> 0, of which waited for: 2 -> 0; matrix products, arithmetic and copies ran while one was open for 2% -> 0% of each run, Pallas kernels for 0% -> 0%
where the time goes in v1:
time: 39.9 us; the launch traced here: 39.7 us
  Pallas kernels  37.1 us (93%)
  local copies, waits for them, and re-layouts  1.89 us (5%)
  between operations  0.65 us (2%)
    pallas_call x1, Pallas kernels, body(): pl.pallas_call(kernel, out_shape=(jax.ShapeDtypeStruct((64, 128), F32), j...  37.1 us
    unnamed x4, local copies, waits for them, and re-layouts  1.89 us

profile of v1, /device:TPU:1, one launch (start us, length us, event | category | flops | bytes accessed | tf_op | source)
XLA Modules:
  0.0 39.7 jit_solution(17403746815096683367)
XLA Ops:
  0.6 37.1 %shard_map.68 = (f32[64,128]{1,0:T(8,128)}, f32[1,64]{1,0:T(1,128)}) custom-call(f32[64,128]{1,0:T(8,128)} %q_ref.1, f32[3,64,128]{2,1,0:T(8,128)} %bitcast.4, f32[64,128]{1,0:T(8,128)} %wid_ref.1, s32[1,64]{1,0:T(1,128)} %bitcast.6, s32[3,256]{1,0:T(4,128)} %bitcast.5), custom_call_target="tpu_custom_call" | custom-call | tf_op jit(solution)/shard_map/pallas_call | solution.py:310
  37.8 0.0 copy-start
  37.8 1.4 %copy.9 = f32[64,128]{1,0:T(8,128)} copy(f32[64,128]{1,0:T(8,128)} %get-tuple-element.8) | data formatting | bytes 65536
  39.2 0.0 copy-done
  39.2 0.5 %copy.10 = f32[64]{0:T(128)} copy(f32[64]{0:T(128)S(1)} %bitcast.7) | data formatting | bytes 512
Async XLA Ops:
  37.8 1.4 %copy-start = (f32[1,64]{1,0:T(1,128)S(1)}, f32[1,64]{1,0:T(1,128)}, u32[]{:S(2)}) copy-start(f32[1,64]{1,0:T(1,128)} %get-tuple-element.5) | copy-start | bytes 772

commit v2 on v1

--- a/solution.py
+++ b/solution.py
@@ -65,75 +65,123 @@
     box = iota((64, 128), 0)
     cells = (box // 16, box // 4 % 4, box % 4)
     norm = wid_ref[...]
-    one, zero = jnp.ones((64, 128), F32), jnp.zeros((64, 128), F32)
+    one = jnp.ones((64, 128), F32)
     for c in range(3):
         x = pos_ref[c] + (cells[c].astype(F32) - 2.0)
         norm = norm + x * x
-        left_ref[c] = -2.0 * x
-        right_ref[c] = x
-    left_ref[3], right_ref[3] = norm, one
-    left_ref[4], right_ref[4] = one, norm
-    for c in range(5, 8):
-        left_ref[c] = zero
-        right_ref[c] = zero
-
-
-def features(r, left_ref, right_ref, ql_ref, lt_ref, rt_ref, qc_ref):
+        left_ref[64 * c : 64 * c + 64] = -2.0 * x
+        right_ref[64 * c : 64 * c + 64] = x
+    left_ref[192:256], right_ref[192:256] = norm, one
+    left_ref[256:320], right_ref[256:320] = one, norm
+    left_ref[320:512] = jnp.zeros((192, 128), F32)
+    right_ref[320:512] = jnp.zeros((192, 128), F32)
+
+
+def features(g, left_ref, right_ref, ql_ref, lt_ref, rt_ref, qc_ref):
     eye = jnp.where(iota((128, 128), 0) == iota((128, 128), 1), 1.0, 0.0).astype(BF16)
     pad = jnp.zeros((128 - DEPTH, 128), BF16)
     packed = []
-    for k in range(4):
-        b = 4 * r + k
-        h, m, l = split3(left_ref[:, b, :])
+    for k in range(8):
+        b = 8 * g + k
+        h, m, l = split3(left_ref[pl.ds(b, 8, stride=64), :])
         packed.append(jnp.concatenate([h, h, m, m, h, l], axis=0).astype(BF16))
-        h, m, l = split3(right_ref[:, b, :])
-        rt_ref[r, :, 128 * k : 128 * k + 128] = jnp.concatenate([h, m, h, m, l, h], axis=0).astype(BF16)
-    for k in (0, 2):
+        h, m, l = split3(right_ref[pl.ds(b, 8, stride=64), :])
+        lanes = slice(128 * (k % 4), 128 * (k % 4) + 128)
+        rt_ref[2 * g + k // 4, :, lanes] = jnp.concatenate([h, m, h, m, l, h], axis=0).astype(BF16)
+    for k in range(0, 8, 2):
         t = dot_nt(eye, jnp.concatenate([packed[k], pad, packed[k + 1], pad], axis=0))
         for kk in (0, 1):
-            lt_ref[rows((4 * r + k + kk) * 128, 128), :] = t[:, 128 * kk : 128 * kk + DEPTH].astype(BF16)
-    for k in range(4):
-        b = 4 * r + k
-        h, m, l = split3(jnp.broadcast_to(ql_ref[pl.ds(b, 1), :], (128, 128)))
-        t = dot_nt(eye, h.astype(BF16)) + dot_nt(eye, m.astype(BF16)) + dot_nt(eye, l.astype(BF16))
-        qc_ref[rows(b * 128, 128), :] = t
-
-
-def kernel_block(r1, ka, r2, lo, hi, lt_ref, rt_ref):
-    left = lt_ref[rows(r1 * 512 + ka * 128, 128), :]
-    d = dot(left, rt_ref[r2, :, lo * 128 : (hi + 1) * 128])
-    return lax.rsqrt(d) - lax.rsqrt(d + SOFT_TERM)
-
-
-def produce(r1, r2, slot, lt_ref, rt_ref, k_ref):
-    for ka in range(4):
-        lo, hi = span(ka)
-        k_ref[slot, ka, :, lo * 128 : (hi + 1) * 128] = kernel_block(r1, ka, r2, lo, hi, lt_ref, rt_ref)
-
-
-def consume(r1, r2, block, spans, ql_ref, qc_ref, cnt_ref, acc1_ref, acc2_ref, diff):
-    crow = cnt_ref[pl.ds(r1, 1), :]
-    back = {}
-    for ka, (lo, hi) in spans:
-        k = block(ka)
+            lt_ref[rows((8 * g + k + kk) * 128, 128), :] = t[:, 128 * kk : 128 * kk + DEPTH].astype(BF16)
+    q = ql_ref[rows(8 * g, 8), :].T
+    for k in range(8):
+        qc_ref[rows((8 * g + k) * 128, 128), :] = jnp.broadcast_to(q[:, k : k + 1], (128, 128))
+
+
+CROSS = [(ka, kb) for ka in range(4) for kb in range(span(ka)[0], span(ka)[1] + 1)]
+OWN = [(ka, ka + 1) for ka in range(3)]
+PAIRS = 42
+
+
+def produce(r1, r2, spans, index, lt_ref, rt_ref, qc_ref, k_ref, back_ref):
+    for ka, lo, hi in spans:
+        left = lt_ref[rows(r1 * 512 + ka * 128, 128), :]
+        d = dot(left, rt_ref[r2, :, lo * 128 : (hi + 1) * 128])
+        kern = lax.rsqrt(d) - lax.rsqrt(d + SOFT_TERM)
         qc = qc_ref[rows(r1 * 512 + ka * 128, 128), :].reshape(16, 8, 128)
-        total = None
         for kb in range(lo, hi + 1):
+            kk = kern[:, (kb - lo) * 128 : (kb - lo + 1) * 128]
+            k_ref[index(ka, kb)] = kk
+            back_ref[index(ka, kb)] = jnp.sum(kk.reshape(16, 8, 128) * qc, axis=0)
+
+
+CROSS_SPANS = [(ka, *span(ka)) for ka in range(4)]
+OWN_SPANS = [(ka, ka + 1, ka + 1) for ka in range(3)]
+
+
+def cross_index(slot):
+    return lambda ka, kb: slot * len(CROSS) + CROSS.index((ka, kb))
+
+
+def own_index(row):
+    return lambda ka, kb: PAIRS * len(CROSS) + row * len(OWN) + ka
+
+
+def produce_three(t, *refs):
+    g4, g7, g10 = (t + 10) // 14, t // 7, t // 10
+    i = t - 4 * g4 - 3 * g7 - 3 * g10
+    base = 4 * i + g4 - g7 - i * g10
+    diff = 1 + 2 * g4 + 2 * g7 - g10
+    for j in range(3):
+        produce(base + j, base + j + diff, CROSS_SPANS, cross_index(3 * t + j), *refs)
+
+
+def produce_own(t, *refs):
+    for j in range(4):
+        r = 4 * t + j
+        produce(r, r, OWN_SPANS, own_index(r), *refs)
+
+
+def consume(r1, parts, ql_ref, cnt_ref, k_ref, back_ref, col_ref, acc_ref):
+    crow = jnp.broadcast_to(cnt_ref[pl.ds(r1, 1), :], (8, 128))
+    lanes = iota((128, 128), 1)
+    totals = [None] * 4
+    for diff, pairs, index in parts:
+        back = {}
+        for ka, kb in pairs:
             lane = diff * 16 + 4 * ka + kb
             c = jnp.broadcast_to(crow[:, lane : lane + 1], (8, 128))
-            kk = k[:, (kb - lo) * 128 : (kb - lo + 1) * 128].reshape(16, 8, 128)
-            cq = c * jnp.broadcast_to(ql_ref[pl.ds(4 * r2 + kb, 1), :], (8, 128))
-            part = kk * cq[None]
-            total = part if total is None else total + part
-            b = jnp.sum(kk * qc, axis=0) * c
+            cq = c * jnp.broadcast_to(ql_ref[pl.ds(4 * (r1 + diff) + kb, 1), :], (8, 128))
+            part = k_ref[index(ka, kb)].reshape(16, 8, 128) * cq[None]
+            totals[ka] = part if totals[ka] is None else totals[ka] + part
+            b = back_ref[index(ka, kb)] * c
             back[kb] = b if kb not in back else back[kb] + b
-        acc1_ref[4 * r1 + ka] += total.reshape(128, 128)
-    for kb, b in back.items():
-        acc2_ref[4 * r2 + kb] += b
-
-
-CROSS = [(ka, span(ka)) for ka in range(4)]
-OWN = [(ka, (ka + 1, ka + 1)) for ka in range(3)]
+        for kb, b in back.items():
+            acc_ref[rows((4 * (r1 + diff) + kb) * 8, 8), :] += b
+    for ka in range(4):
+        if totals[ka] is not None:
+            total = jnp.sum(totals[ka].reshape(128, 128), axis=1, keepdims=True)
+            col_ref[...] = jnp.where(lanes == 4 * r1 + ka, total, col_ref[...])
+
+
+def consume_all(*refs):
+    def step(i, carry):
+        for j in range(4):
+            r1 = 4 * i + j
+            parts = [(0, OWN, own_index(r1)), (4, CROSS, cross_index(30 + r1))]
+            if j <= 2:
+                parts.append((1, CROSS, cross_index(3 * i + j)))
+                parts.append((5, CROSS, cross_index(21 + 3 * i + j)))
+            if j >= 1:
+                parts.append((3, CROSS, cross_index(12 + 3 * i + j - 1)))
+            consume(r1, parts, *refs)
+        return carry
+
+    lax.fori_loop(0, 3, step, 0)
+    for j in range(4):
+        parts = [(0, OWN, own_index(12 + j))]
+        if j <= 2:
+            parts.append((1, CROSS, cross_index(9 + j)))
+        consume(12 + j, parts, *refs)
 
 
 def count_pairs(got, cnt_ref):
@@ -165,30 +213,17 @@
     return jnp.sum(jnp.where(eye, col, 0.0), axis=0, keepdims=True)
 
 
-def collect(acc1_ref, acc2_ref, live, out_ref):
-    row = iota((16, 128), 0)
-
-    def step(g, carry):
-        total = jnp.zeros((16, 128), F32)
-        for k in range(8):
-            b = 8 * g + k
-            x = acc1_ref[b]
-            h = x.astype(BF16)
-            low = (x - h.astype(F32)).astype(BF16)
-            pick = jnp.where(row == k, 1.0, 0.0).astype(BF16)
-            total = total + dot_nt(pick, h) + dot_nt(pick, low)
-            s = jnp.sum(acc2_ref[b], axis=0, keepdims=True)
-            total = total + jnp.where(row == k, s, 0.0)
-        out_ref[rows(8 * g, 8), :] = total[:8]
-        return carry
-
-    lax.fori_loop(0, 8, step, 0)
-    out_ref[...] = jnp.where(live, out_ref[...], 0.0)
+def collect(col_ref, acc_ref, live, out_ref):
+    total = col_ref[...].T[:64]
+    for sub in range(8):
+        part = [acc_ref[pl.ds(64 * g + sub, 8, stride=8), :] for g in range(8)]
+        total = total + jnp.concatenate(part, axis=0)
+    out_ref[...] = jnp.where(live, total, 0.0)
 
 
 def kernel(
     q_ref, pos_ref, wid_ref, cnt_ref, rec_ref, near_ref, far_ref,
-    left_ref, right_ref, lt_ref, rt_ref, ql_ref, qc_ref, k_ref, c_ref, acc1_ref, acc2_ref,
+    left_ref, right_ref, lt_ref, rt_ref, ql_ref, qc_ref, k_ref, back_ref, c_ref, col_ref, acc_ref,
     send_ref, mid_ref, turn_ref, got_ref, send1, recv1, send2, recv2,
 ):
     u, v = lax.axis_index("gx"), lax.axis_index("gy")
@@ -204,8 +239,31 @@
     live = iota((64, 128), 1) < cnt
     ql_ref[...] = jnp.where(live, q_ref[...], 0.0)
     messages(rec_ref, ql_ref, send_ref)
+
+    later = 4 * (v % 4) + 5 * (v // 4) + 8 * (u // 2)
+    early = jnp.maximum(0, 52 - later)
+    features_first = jnp.minimum(4, early // 5)
+    pairs_first = jnp.maximum(0, early - 12) // 7
+    pairs_second = pairs_first + 1 + jnp.minimum(early, 12) // 12
+
+    def feature_step(t, carry):
+        for g in range(2):
+            features(2 * t + g, left_ref, right_ref, ql_ref, lt_ref, rt_ref, qc_ref)
+        return carry
+
+    def produce_step(t, carry):
+        produce_three(t, lt_ref, rt_ref, qc_ref, k_ref, back_ref)
+        return carry
+
+    def own_step(t, carry):
+        produce_own(t, lt_ref, rt_ref, qc_ref, k_ref, back_ref)
+        return carry
+
+    planes(pos_ref, wid_ref, left_ref, right_ref)
+    lax.fori_loop(0, features_first, feature_step, 0)
+    lax.fori_loop(0, pairs_first, produce_step, 0)
+
     pl.semaphore_wait(barrier, GX + GY - 2)
-
     first = [
         pltpu.make_async_remote_copy(
             src_ref=send_ref.at[rows(x * GY, GY)],
@@ -221,15 +279,8 @@
         copy.start()
     mid_ref[rows(u * GY, GY), :] = send_ref[rows(u * GY, GY), :]
 
-    acc1_ref[...] = jnp.zeros_like(acc1_ref)
-    acc2_ref[...] = jnp.zeros_like(acc2_ref)
-    planes(pos_ref, wid_ref, left_ref, right_ref)
-
-    def feature_step(r, carry):
-        features(r, left_ref, right_ref, ql_ref, lt_ref, rt_ref, qc_ref)
-        return carry
-
-    lax.fori_loop(0, 16, feature_step, 0)
+    lax.fori_loop(features_first, 4, feature_step, 0)
+    lax.fori_loop(pairs_first, pairs_second, produce_step, 0)
 
     for copy in first:
         copy.wait_recv()
@@ -250,57 +301,18 @@
         copy.start()
     got_ref[rows(v * GX, GX), :] = turn_ref[rows(v * GX, GX), :]
 
-    def produce_step(i, carry):
-        for j in range(3):
-            produce(4 * i + j, 4 * i + j + 1, 3 * i + j, lt_ref, rt_ref, k_ref)
-        return carry
-
-    lax.fori_loop(0, 4, produce_step, 0)
+    lax.fori_loop(pairs_second, PAIRS // 3, produce_step, 0)
+    lax.fori_loop(0, 4, own_step, 0)
+    acc_ref[...] = jnp.zeros_like(acc_ref)
+    col_ref[...] = jnp.zeros_like(col_ref)
 
     for copy in second:
         copy.wait_recv()
     got = got_ref[...].T
     count_pairs(got, c_ref)
     far_ref[...] = far_field(got, u, v)
-
-    sums = (ql_ref, qc_ref, c_ref, acc1_ref, acc2_ref)
-
-    def direct(r1, diff, spans):
-        r2, of = r1 + diff, dict(spans)
-        consume(r1, r2, lambda ka: kernel_block(r1, ka, r2, *of[ka], lt_ref, rt_ref), spans, *sums, diff)
-
-    for dj in (-1, 1):
-
-        def diagonal_step(i, carry, dj=dj):
-            for j in range(3):
-                direct(4 * i + j + (dj < 0), 4 + dj, CROSS)
-            return carry
-
-        lax.fori_loop(0, 3, diagonal_step, 0)
-
-    def straight_step(i, carry):
-        for j in range(4):
-            p = 4 * i + j
-            direct(p, 4, CROSS)
-
-            def block(ka, p=p):
-                lo, hi = span(ka)
-                return k_ref[p, ka, :, lo * 128 : (hi + 1) * 128]
-
-            r1 = p // 3 * 4 + p % 3
-            consume(r1, r1 + 1, block, CROSS, *sums, 1)
-        return carry
-
-    lax.fori_loop(0, 3, straight_step, 0)
-
-    def own_step(i, carry):
-        for j in range(4):
-            direct(4 * i + j, 0, OWN)
-        return carry
-
-    lax.fori_loop(0, 4, own_step, 0)
-
-    collect(acc1_ref, acc2_ref, live, near_ref)
+    consume_all(ql_ref, c_ref, k_ref, back_ref, col_ref, acc_ref)
+    collect(col_ref, acc_ref, live, near_ref)
     for copy in first + second:
         copy.wait_send()
 
@@ -313,16 +325,17 @@
         in_specs=[pl.BlockSpec(memory_space=vmem)] * 5,
         out_specs=(pl.BlockSpec(memory_space=vmem),) * 2,
         scratch_shapes=[
-            vmem((8, 64, 128), F32),
-            vmem((8, 64, 128), F32),
+            vmem((512, 128), F32),
+            vmem((512, 128), F32),
             vmem((8192, DEPTH), BF16),
             vmem((16, DEPTH, 512), BF16),
             vmem((64, 128), F32),
             vmem((8192, 128), F32),
-            vmem((12, 4, 128, 512), F32),
+            vmem((468, 128, 128), F32),
+            vmem((468, 8, 128), F32),
             vmem((16, 128), F32),
-            vmem((64, 128, 128), F32),
-            vmem((64, 8, 128), F32),
+            vmem((128, 128), F32),
+            vmem((512, 128), F32),
             vmem((DEVICES, 128), F32),
             vmem((DEVICES, 128), F32),
             vmem((DEVICES, 128), F32),

time: 39.9 us -> 28.3 us (0.71)
  Pallas kernels: 37.1 us -> 25.6 us
    pallas_call x1, Pallas kernels: 37.1 us -> 25.6 us  [body(): pl.pallas_call(kernel, out_shape=(jax.ShapeDtypeStruct((64, 128), F32), j...]
where the time goes in v2:
time: 28.3 us; the launch traced here: 28.1 us
  Pallas kernels  25.6 us (90%)
  local copies, waits for them, and re-layouts  1.89 us (7%)
  between operations  0.65 us (2%)
    pallas_call x1, Pallas kernels, body(): pl.pallas_call(kernel, out_shape=(jax.ShapeDtypeStruct((64, 128), F32), j...  25.6 us
    unnamed x4, local copies, waits for them, and re-layouts  1.89 us

profile of v2, /device:TPU:1, one launch (start us, length us, event | category | flops | bytes accessed | tf_op | source)
XLA Modules:
  0.0 28.1 jit_solution(3480344171419002516)
XLA Ops:
  0.6 25.6 %shard_map.68 = (f32[64,128]{1,0:T(8,128)}, f32[1,64]{1,0:T(1,128)}) custom-call(f32[64,128]{1,0:T(8,128)} %q_ref.1, f32[3,64,128]{2,1,0:T(8,128)} %bitcast.4, f32[64,128]{1,0:T(8,128)} %wid_ref.1, s32[1,64]{1,0:T(1,128)} %bitcast.6, s32[3,256]{1,0:T(4,128)} %bitcast.5), custom_call_target="tpu_custom_call" | custom-call | tf_op jit(solution)/shard_map/pallas_call | solution.py:322
  26.2 0.0 copy-start
  26.2 1.4 %copy.9 = f32[64,128]{1,0:T(8,128)} copy(f32[64,128]{1,0:T(8,128)} %get-tuple-element.8) | data formatting | bytes 65536
  27.6 0.0 copy-done
  27.6 0.5 %copy.10 = f32[64]{0:T(128)} copy(f32[64]{0:T(128)S(1)} %bitcast.7) | data formatting | bytes 512
Async XLA Ops:
  26.2 1.4 %copy-start = (f32[1,64]{1,0:T(1,128)S(1)}, f32[1,64]{1,0:T(1,128)}, u32[]{:S(2)}) copy-start(f32[1,64]{1,0:T(1,128)} %get-tuple-element.5) | copy-start | bytes 772

commit v3 on v2

--- a/solution.py
+++ b/solution.py
@@ -222,11 +222,15 @@
 
 
 def kernel(
-    q_ref, pos_ref, wid_ref, cnt_ref, rec_ref, near_ref, far_ref,
+    q_hbm, pos_hbm, wid_hbm, cnt_hbm, rec_hbm, near_ref, far_ref, q_ref, pos_ref, wid_ref, cnt_ref, rec_ref, in_sem,
     left_ref, right_ref, lt_ref, rt_ref, ql_ref, qc_ref, k_ref, back_ref, c_ref, col_ref, acc_ref,
     send_ref, mid_ref, turn_ref, got_ref, send1, recv1, send2, recv2,
 ):
     u, v = lax.axis_index("gx"), lax.axis_index("gy")
+    pairs = ((rec_hbm, rec_ref), (cnt_hbm, cnt_ref), (q_hbm, q_ref), (pos_hbm, pos_ref), (wid_hbm, wid_ref))
+    inputs = [pltpu.make_async_copy(a, b, in_sem.at[s]) for s, (a, b) in enumerate(pairs)]
+    for copy in inputs:
+        copy.start()
     others_x = [lax.rem(u + s, GX) for s in range(1, GX)]
     others_y = [lax.rem(v + s, GY) for s in range(1, GY)]
     barrier = pltpu.get_barrier_semaphore()
@@ -235,16 +239,21 @@
     for y in others_y:
         pl.semaphore_signal(barrier, inc=1, device_id=(u, y), device_id_type=MESH)
 
+    for copy in inputs[:3]:
+        copy.wait()
     cnt = column(cnt_ref[...].astype(F32)).astype(I32)
     live = iota((64, 128), 1) < cnt
     ql_ref[...] = jnp.where(live, q_ref[...], 0.0)
     messages(rec_ref, ql_ref, send_ref)
 
-    later = 4 * (v % 4) + 5 * (v // 4) + 8 * (u // 2)
-    early = jnp.maximum(0, 52 - later)
-    features_first = jnp.minimum(4, early // 5)
-    pairs_first = jnp.maximum(0, early - 12) // 7
-    pairs_second = pairs_first + 1 + jnp.minimum(early, 12) // 12
+    wave = 40 * (v % 4) + 48 * (v // 4)
+    enter = 100 + wave + 82 * (u // 2)
+    all_in = 100 + jnp.maximum(246 + wave, 264 + 82 * (u // 2)) + 150
+    crossed = 1110
+    ready = enter + 80
+    features_first = jnp.clip((all_in - ready) // 50, 0, 4)
+    pairs_first = jnp.clip((all_in - ready - 200) // 65, 0, 14)
+    pairs_second = jnp.clip((crossed - ready - 200) // 65, pairs_first, 14)
 
     def feature_step(t, carry):
         for g in range(2):
@@ -259,6 +268,8 @@
         produce_own(t, lt_ref, rt_ref, qc_ref, k_ref, back_ref)
         return carry
 
+    for copy in inputs[3:]:
+        copy.wait()
     planes(pos_ref, wid_ref, left_ref, right_ref)
     lax.fori_loop(0, features_first, feature_step, 0)
     lax.fori_loop(0, pairs_first, produce_step, 0)
@@ -321,10 +332,16 @@
     vmem = pltpu.VMEM
     near, far = pl.pallas_call(
         kernel,
-        out_shape=(jax.ShapeDtypeStruct((64, 128), F32), jax.ShapeDtypeStruct((1, 64), F32)),
-        in_specs=[pl.BlockSpec(memory_space=vmem)] * 5,
+        out_shape=(vmem((64, 128), F32), vmem((1, 64), F32)),
+        in_specs=[pl.BlockSpec(memory_space=pl.ANY)] * 5,
         out_specs=(pl.BlockSpec(memory_space=vmem),) * 2,
         scratch_shapes=[
+            vmem((64, 128), F32),
+            vmem((3, 64, 128), F32),
+            vmem((64, 128), F32),
+            vmem((1, 64), I32),
+            vmem((3, 256), I32),
+            pltpu.SemaphoreType.DMA((5,)),
             vmem((512, 128), F32),
             vmem((512, 128), F32),
             vmem((8192, DEPTH), BF16),

time: 28.3 us -> 23.7 us (0.84)
  Pallas kernels: 25.6 us -> 21.8 us
  local copies, waits for them, and re-layouts: 1.89 us -> 1.13 us
    pallas_call x1, Pallas kernels: 25.6 us -> 21.8 us  [body(): pl.pallas_call(kernel, out_shape=(vmem((64, 128), F32), vmem((1, 64), F32...]
    unnamed x4 -> x2, local copies, waits for them, and re-layouts: 1.89 us -> 1.13 us
where the time goes in v3:
time: 23.7 us; the launch traced here: 23.6 us
  Pallas kernels  21.8 us (92%)
  local copies, waits for them, and re-layouts  1.13 us (5%)
  between operations  0.64 us (3%)
    pallas_call x1, Pallas kernels, body(): pl.pallas_call(kernel, out_shape=(vmem((64, 128), F32), vmem((1, 64), F32...  21.8 us
    unnamed x2, local copies, waits for them, and re-layouts  1.13 us

profile of v3, /device:TPU:1, one launch (start us, length us, event | category | flops | bytes accessed | tf_op | source)
XLA Modules:
  0.0 23.6 jit_solution(10273758044448304469)
XLA Ops:
  0.6 21.8 %shard_map.68 = (f32[64,128]{1,0:T(8,128)S(1)}, f32[1,64]{1,0:T(1,128)S(1)}) custom-call(f32[64,128]{1,0:T(8,128)} %q_hbm.1, f32[3,64,128]{2,1,0:T(8,128)} %bitcast.5, f32[64,128]{1,0:T(8,128)} %wid_hbm.1, s32[1,64]{1,0:T(1,128)} %bitcast.7, s32[3,256]{1,0:T(4,128)} %bitcast.6), custom_call_target="tpu_custom_call" | custom-call | tf_op jit(solution)/shard_map/pallas_call | solution.py:333
  22.5 0.6 %copy.9 = f32[64,128]{1,0:T(8,128)} copy(f32[64,128]{1,0:T(8,128)S(1)} %get-tuple-element.6) | data formatting | bytes 65536
  23.1 0.5 %copy.10 = f32[64]{0:T(128)} copy(f32[64]{0:T(128)S(1)} %bitcast.4) | data formatting | bytes 512

commit v4 on v3

--- a/solution.py
+++ b/solution.py
@@ -11,6 +11,7 @@
 DEVICES = GX * GY
 DEPTH = 48
 SOFT_TERM = 2.0
+FEATURE_TIME, STEP_TIME = 150, 136
 
 
 def iota(shape, dim):
@@ -97,12 +98,20 @@
         qc_ref[rows((8 * g + k) * 128, 128), :] = jnp.broadcast_to(q[:, k : k + 1], (128, 128))
 
 
-CROSS = [(ka, kb) for ka in range(4) for kb in range(span(ka)[0], span(ka)[1] + 1)]
-OWN = [(ka, ka + 1) for ka in range(3)]
+CROSS_SPANS = [(ka, *span(ka)) for ka in range(4)]
+OWN_SPANS = [(ka, ka + 1, ka + 1) for ka in range(3)]
 PAIRS = 42
-
-
-def produce(r1, r2, spans, index, lt_ref, rt_ref, qc_ref, k_ref, back_ref):
+TRIPLES = 2
+STEPS = 14 // TRIPLES
+
+
+def key_of(kind, ka, kb):
+    return 32 * ka + 4 * kind + kb
+
+
+def produce(r1, r2, kind, slot, spans, back, ql_ref, qc_ref, lt_ref, rt_ref, set_ref, back_ref):
+    lanes = iota((128, 128), 1) - 4 * kind
+    tile = None
     for ka, lo, hi in spans:
         left = lt_ref[rows(r1 * 512 + ka * 128, 128), :]
         d = dot(left, rt_ref[r2, :, lo * 128 : (hi + 1) * 128])
@@ -110,91 +119,109 @@
         qc = qc_ref[rows(r1 * 512 + ka * 128, 128), :].reshape(16, 8, 128)
         for kb in range(lo, hi + 1):
             kk = kern[:, (kb - lo) * 128 : (kb - lo + 1) * 128]
-            k_ref[index(ka, kb)] = kk
-            back_ref[index(ka, kb)] = jnp.sum(kk.reshape(16, 8, 128) * qc, axis=0)
-
-
-CROSS_SPANS = [(ka, *span(ka)) for ka in range(4)]
-OWN_SPANS = [(ka, ka + 1, ka + 1) for ka in range(3)]
-
-
-def cross_index(slot):
-    return lambda ka, kb: slot * len(CROSS) + CROSS.index((ka, kb))
-
-
-def own_index(row):
-    return lambda ka, kb: PAIRS * len(CROSS) + row * len(OWN) + ka
-
-
-def produce_three(t, *refs):
-    g4, g7, g10 = (t + 10) // 14, t // 7, t // 10
+            back_ref[back(ka, kb)] = jnp.sum(kk.reshape(16, 8, 128) * qc, axis=0)
+            x = jnp.sum(kk * ql_ref[pl.ds(4 * r2 + kb, 1), :], axis=1, keepdims=True)
+            tile = jnp.broadcast_to(x, (128, 128)) if tile is None else jnp.where(lanes == key_of(0, ka, kb), x, tile)
+    set_ref[slot] = tile
+
+
+def cross_back(slot):
+    return lambda ka, kb: slot * 10 + 3 * ka - 1 * (ka > 0) + kb - span(ka)[0]
+
+
+def own_back(row):
+    return lambda ka, kb: PAIRS * 10 + row * 3 + ka
+
+
+def step_rows(t):
+    g4, g7, g10 = (t + 28) // 32, (t + 25) // 32, (t + 22) // 32
     i = t - 4 * g4 - 3 * g7 - 3 * g10
-    base = 4 * i + g4 - g7 - i * g10
-    diff = 1 + 2 * g4 + 2 * g7 - g10
-    for j in range(3):
-        produce(base + j, base + j + diff, CROSS_SPANS, cross_index(3 * t + j), *refs)
-
-
-def produce_own(t, *refs):
-    for j in range(4):
-        r = 4 * t + j
-        produce(r, r, OWN_SPANS, own_index(r), *refs)
-
-
-def consume(r1, parts, ql_ref, cnt_ref, k_ref, back_ref, col_ref, acc_ref):
-    crow = jnp.broadcast_to(cnt_ref[pl.ds(r1, 1), :], (8, 128))
-    lanes = iota((128, 128), 1)
-    totals = [None] * 4
-    for diff, pairs, index in parts:
-        back = {}
-        for ka, kb in pairs:
-            lane = diff * 16 + 4 * ka + kb
-            c = jnp.broadcast_to(crow[:, lane : lane + 1], (8, 128))
-            cq = c * jnp.broadcast_to(ql_ref[pl.ds(4 * (r1 + diff) + kb, 1), :], (8, 128))
-            part = k_ref[index(ka, kb)].reshape(16, 8, 128) * cq[None]
-            totals[ka] = part if totals[ka] is None else totals[ka] + part
-            b = back_ref[index(ka, kb)] * c
-            back[kb] = b if kb not in back else back[kb] + b
-        for kb, b in back.items():
-            acc_ref[rows((4 * (r1 + diff) + kb) * 8, 8), :] += b
-    for ka in range(4):
-        if totals[ka] is not None:
-            total = jnp.sum(totals[ka].reshape(128, 128), axis=1, keepdims=True)
-            col_ref[...] = jnp.where(lanes == 4 * r1 + ka, total, col_ref[...])
-
-
-def consume_all(*refs):
+    return 4 * i + g4 - g7 - i * g10, 1 + 2 * g4 + 2 * g7 - g10, g4 + g7 + g10
+
+
+def produce_own(r, refs):
+    produce(r, r, 4, PAIRS + r, OWN_SPANS, own_back(r), *refs)
+
+
+def produce_step(step, refs):
+    for n in range(TRIPLES):
+        t = TRIPLES * step + n
+        base, diff, kind = step_rows(t)
+        for j in range(3):
+            produce(base + j, base + j + diff, kind, 3 * t + j, CROSS_SPANS, cross_back(3 * t + j), *refs)
+        produce_own(t, refs)
+
+
+def row_parts(i, j):
+    inner = not (isinstance(i, int) and i == 3)
+    parts = [(4, 0, PAIRS + 4 * i + j)]
+    if j <= 2:
+        parts.append((0, 1, 3 * i + j))
+    if inner:
+        parts.append((3, 4, 30 + 4 * i + j))
+    if inner and j <= 2:
+        parts.append((2, 5, 21 + 3 * i + j))
+    if inner and j >= 1:
+        parts.append((1, 3, 12 + 3 * i + j - 1))
+    return parts
+
+
+def turn_sets(set_ref, turned_ref):
+    kinds = iota((128, 128), 1) % 32 // 4
+
+    def step(i, carry):
+        for j in range(4):
+            tile = jnp.zeros((128, 128), F32)
+            for kind, _, slot in row_parts(i, j):
+                tile = jnp.where(kinds == kind, set_ref[slot], tile)
+            turned_ref[4 * i + j] = tile.T
+        return carry
+
+    lax.fori_loop(0, 3, step, 0)
+    step(3, 0)
+
+
+def count_pairs(got, key_ref, row_ref):
+    by_key, by_row = jnp.zeros((128, 128), F32), jnp.zeros((16, 128), F32)
+    for k in range(CAP):
+        a, b = got[k : k + 1].astype(I32) - 1, got[CAP + k : CAP + 1 + k].astype(I32) - 1
+        first, second = jnp.minimum(a, b), jnp.maximum(a, b)
+        r1, diff = first // 4, second // 4 - first // 4
+        kind = jnp.where(diff == 0, 4, jnp.where(diff == 1, 0, jnp.where(diff == 3, 1, jnp.where(diff == 5, 2, 3))))
+        key = jnp.where(first >= 0, 32 * (first % 4) + 4 * kind + second % 4, 128)
+        hot_key = jnp.where(iota((128, 128), 0) == key, 1.0, 0.0).astype(BF16)
+        hot_row = jnp.where(iota((16, 128), 0) == r1, 1.0, 0.0).astype(BF16)
+        by_row = by_row + dot_nt(hot_row, hot_key)
+        by_key = by_key + dot_nt(hot_key, jnp.concatenate([hot_row, jnp.zeros((112, 128), BF16)], axis=0))
+    key_ref[...] = by_key
+    for r in range(16):
+        row_ref[8 * r : 8 * r + 8, :] = jnp.broadcast_to(by_row[r : r + 1], (8, 128))
+
+
+def weigh(key_ref, row_ref, turned_ref, back_ref, acc_ref):
+    for r in range(16):
+        weighted = turned_ref[r] * jnp.broadcast_to(key_ref[:, r : r + 1], (128, 128))
+        for ka in range(4):
+            acc_ref[32 * r + 8 * ka : 32 * r + 8 * ka + 8, :] = jnp.sum(weighted[32 * ka : 32 * ka + 32].reshape(4, 8, 128), axis=0)
+
     def step(i, carry):
         for j in range(4):
             r1 = 4 * i + j
-            parts = [(0, OWN, own_index(r1)), (4, CROSS, cross_index(30 + r1))]
-            if j <= 2:
-                parts.append((1, CROSS, cross_index(3 * i + j)))
-                parts.append((5, CROSS, cross_index(21 + 3 * i + j)))
-            if j >= 1:
-                parts.append((3, CROSS, cross_index(12 + 3 * i + j - 1)))
-            consume(r1, parts, *refs)
+            counts = row_ref[rows(8 * r1, 8), :]
+            for kind, diff, slot in row_parts(i, j):
+                sums = {}
+                for ka, lo, hi in OWN_SPANS if kind == 4 else CROSS_SPANS:
+                    for kb in range(lo, hi + 1):
+                        key = key_of(kind, ka, kb)
+                        back = own_back(r1) if kind == 4 else cross_back(slot)
+                        b = back_ref[back(ka, kb)] * jnp.broadcast_to(counts[:, key : key + 1], (8, 128))
+                        sums[kb] = b if kb not in sums else sums[kb] + b
+                for kb, b in sums.items():
+                    acc_ref[rows((4 * (r1 + diff) + kb) * 8, 8), :] += b
         return carry
 
     lax.fori_loop(0, 3, step, 0)
-    for j in range(4):
-        parts = [(0, OWN, own_index(12 + j))]
-        if j <= 2:
-            parts.append((1, CROSS, cross_index(9 + j)))
-        consume(12 + j, parts, *refs)
-
-
-def count_pairs(got, cnt_ref):
-    c = jnp.zeros((16, 128), F32)
-    for k in range(CAP):
-        a, b = got[k : k + 1].astype(I32) - 1, got[CAP + k : CAP + 1 + k].astype(I32) - 1
-        first, second = jnp.minimum(a, b), jnp.maximum(a, b)
-        r1, r2 = first // 4, second // 4
-        lane = (r2 - r1) * 16 + first % 4 * 4 + second % 4
-        hot1 = jnp.where(iota((16, 128), 0) == r1, 1.0, 0.0).astype(BF16)
-        hot2 = jnp.where((iota((128, 128), 0) == lane) & (first >= 0), 1.0, 0.0).astype(BF16)
-        c = c + dot_nt(hot1, hot2)
-    cnt_ref[...] = c
+    step(3, 0)
 
 
 def far_field(got, u, v):
@@ -213,8 +240,8 @@
     return jnp.sum(jnp.where(eye, col, 0.0), axis=0, keepdims=True)
 
 
-def collect(col_ref, acc_ref, live, out_ref):
-    total = col_ref[...].T[:64]
+def collect(acc_ref, live, out_ref):
+    total = jnp.zeros((64, 128), F32)
     for sub in range(8):
         part = [acc_ref[pl.ds(64 * g + sub, 8, stride=8), :] for g in range(8)]
         total = total + jnp.concatenate(part, axis=0)
@@ -223,7 +250,7 @@
 
 def kernel(
     q_hbm, pos_hbm, wid_hbm, cnt_hbm, rec_hbm, near_ref, far_ref, q_ref, pos_ref, wid_ref, cnt_ref, rec_ref, in_sem,
-    left_ref, right_ref, lt_ref, rt_ref, ql_ref, qc_ref, k_ref, back_ref, c_ref, col_ref, acc_ref,
+    left_ref, right_ref, lt_ref, rt_ref, ql_ref, qc_ref, set_ref, turned_ref, back_ref, key_ref, row_ref, acc_ref,
     send_ref, mid_ref, turn_ref, got_ref, send1, recv1, send2, recv2,
 ):
     u, v = lax.axis_index("gx"), lax.axis_index("gy")
@@ -251,30 +278,20 @@
     all_in = 100 + jnp.maximum(246 + wave, 264 + 82 * (u // 2)) + 150
     crossed = 1110
     ready = enter + 80
-    features_first = jnp.clip((all_in - ready) // 50, 0, 4)
-    pairs_first = jnp.clip((all_in - ready - 200) // 65, 0, 14)
-    pairs_second = jnp.clip((crossed - ready - 200) // 65, pairs_first, 14)
-
-    def feature_step(t, carry):
-        for g in range(2):
-            features(2 * t + g, left_ref, right_ref, ql_ref, lt_ref, rt_ref, qc_ref)
+    late = all_in < ready + 100
+    pairs_first = jnp.where(late, 0, jnp.clip((all_in - ready - FEATURE_TIME + STEP_TIME // 2) // STEP_TIME, 0, STEPS))
+    pairs_second = jnp.clip((crossed - ready - FEATURE_TIME + STEP_TIME // 2) // STEP_TIME, pairs_first, STEPS)
+
+    refs = (ql_ref, qc_ref, lt_ref, rt_ref, set_ref, back_ref)
+
+    def pair_step(t, carry):
+        produce_step(t, refs)
         return carry
 
-    def produce_step(t, carry):
-        produce_three(t, lt_ref, rt_ref, qc_ref, k_ref, back_ref)
-        return carry
-
-    def own_step(t, carry):
-        produce_own(t, lt_ref, rt_ref, qc_ref, k_ref, back_ref)
-        return carry
-
-    for copy in inputs[3:]:
-        copy.wait()
-    planes(pos_ref, wid_ref, left_ref, right_ref)
-    lax.fori_loop(0, features_first, feature_step, 0)
-    lax.fori_loop(0, pairs_first, produce_step, 0)
-
-    pl.semaphore_wait(barrier, GX + GY - 2)
+    def make_features():
+        for g in range(8):
+            features(g, left_ref, right_ref, ql_ref, lt_ref, rt_ref, qc_ref)
+
     first = [
         pltpu.make_async_remote_copy(
             src_ref=send_ref.at[rows(x * GY, GY)],
@@ -286,12 +303,21 @@
         )
         for s, x in enumerate(others_x)
     ]
-    for copy in first:
-        copy.start()
+
+    def send_first():
+        pl.semaphore_wait(barrier, GX + GY - 2)
+        for copy in first:
+            copy.start()
+
+    for copy in inputs[3:]:
+        copy.wait()
+    planes(pos_ref, wid_ref, left_ref, right_ref)
     mid_ref[rows(u * GY, GY), :] = send_ref[rows(u * GY, GY), :]
-
-    lax.fori_loop(features_first, 4, feature_step, 0)
-    lax.fori_loop(pairs_first, pairs_second, produce_step, 0)
+    pl.when(late)(send_first)
+    make_features()
+    lax.fori_loop(0, pairs_first, pair_step, 0)
+    pl.when(jnp.logical_not(late))(send_first)
+    lax.fori_loop(pairs_first, pairs_second, pair_step, 0)
 
     for copy in first:
         copy.wait_recv()
@@ -312,18 +338,18 @@
         copy.start()
     got_ref[rows(v * GX, GX), :] = turn_ref[rows(v * GX, GX), :]
 
-    lax.fori_loop(pairs_second, PAIRS // 3, produce_step, 0)
-    lax.fori_loop(0, 4, own_step, 0)
-    acc_ref[...] = jnp.zeros_like(acc_ref)
-    col_ref[...] = jnp.zeros_like(col_ref)
+    lax.fori_loop(pairs_second, STEPS, pair_step, 0)
+    for r in (14, 15):
+        produce_own(r, refs)
+    turn_sets(set_ref, turned_ref)
 
     for copy in second:
         copy.wait_recv()
     got = got_ref[...].T
-    count_pairs(got, c_ref)
+    count_pairs(got, key_ref, row_ref)
     far_ref[...] = far_field(got, u, v)
-    consume_all(ql_ref, c_ref, k_ref, back_ref, col_ref, acc_ref)
-    collect(col_ref, acc_ref, live, near_ref)
+    weigh(key_ref, row_ref, turned_ref, back_ref, acc_ref)
+    collect(acc_ref, live, near_ref)
     for copy in first + second:
         copy.wait_send()
 
@@ -348,9 +374,10 @@
             vmem((16, DEPTH, 512), BF16),
             vmem((64, 128), F32),
             vmem((8192, 128), F32),
-            vmem((468, 128, 128), F32),
+            vmem((PAIRS + 16, 128, 128), F32),
+            vmem((16, 128, 128), F32),
             vmem((468, 8, 128), F32),
-            vmem((16, 128), F32),
+            vmem((128, 128), F32),
             vmem((128, 128), F32),
             vmem((512, 128), F32),
             vmem((DEVICES, 128), F32),

time: 23.7 us -> 21.3 us (0.90)
  Pallas kernels: 21.8 us -> 19.4 us
    pallas_call x1, Pallas kernels: 21.8 us -> 19.4 us  [body(): pl.pallas_call(kernel, out_shape=(vmem((64, 128), F32), vmem((1, 64), F32...]
where the time goes in v4:
time: 21.3 us; the launch traced here: 21.2 us
  Pallas kernels  19.4 us (91%)
  local copies, waits for them, and re-layouts  1.13 us (5%)
  between operations  0.64 us (3%)
    pallas_call x1, Pallas kernels, body(): pl.pallas_call(kernel, out_shape=(vmem((64, 128), F32), vmem((1, 64), F32...  19.4 us
    unnamed x2, local copies, waits for them, and re-layouts  1.13 us

profile of v4, /device:TPU:1, one launch (start us, length us, event | category | flops | bytes accessed | tf_op | source)
XLA Modules:
  0.0 21.2 jit_solution(8231536097505922507)
XLA Ops:
  0.6 19.4 %shard_map.68 = (f32[64,128]{1,0:T(8,128)S(1)}, f32[1,64]{1,0:T(1,128)S(1)}) custom-call(f32[64,128]{1,0:T(8,128)} %q_hbm.1, f32[3,64,128]{2,1,0:T(8,128)} %bitcast.5, f32[64,128]{1,0:T(8,128)} %wid_hbm.1, s32[1,64]{1,0:T(1,128)} %bitcast.7, s32[3,256]{1,0:T(4,128)} %bitcast.6), custom_call_target="tpu_custom_call" | custom-call | tf_op jit(solution)/shard_map/pallas_call | solution.py:359
  20.0 0.6 %copy.9 = f32[64,128]{1,0:T(8,128)} copy(f32[64,128]{1,0:T(8,128)S(1)} %get-tuple-element.6) | data formatting | bytes 65536
  20.6 0.5 %copy.10 = f32[64]{0:T(128)} copy(f32[64]{0:T(128)S(1)} %bitcast.4) | data formatting | bytes 512

commit v5 on v4

--- a/solution.py
+++ b/solution.py
@@ -166,7 +166,7 @@
     return parts
 
 
-def turn_sets(set_ref, turned_ref):
+def turn_sets(set_ref, high_ref, low_ref):
     kinds = iota((128, 128), 1) % 32 // 4
 
     def step(i, carry):
@@ -174,15 +174,18 @@
             tile = jnp.zeros((128, 128), F32)
             for kind, _, slot in row_parts(i, j):
                 tile = jnp.where(kinds == kind, set_ref[slot], tile)
-            turned_ref[4 * i + j] = tile.T
+            tile = tile.T
+            high = tile.astype(BF16)
+            high_ref[4 * i + j] = high
+            low_ref[4 * i + j] = (tile - high.astype(F32)).astype(BF16)
         return carry
 
     lax.fori_loop(0, 3, step, 0)
     step(3, 0)
 
 
-def count_pairs(got, key_ref, row_ref):
-    by_key, by_row = jnp.zeros((128, 128), F32), jnp.zeros((16, 128), F32)
+def count_pairs(got, row_ref):
+    by_row = jnp.zeros((16, 128), F32)
     for k in range(CAP):
         a, b = got[k : k + 1].astype(I32) - 1, got[CAP + k : CAP + 1 + k].astype(I32) - 1
         first, second = jnp.minimum(a, b), jnp.maximum(a, b)
@@ -192,65 +195,71 @@
         hot_key = jnp.where(iota((128, 128), 0) == key, 1.0, 0.0).astype(BF16)
         hot_row = jnp.where(iota((16, 128), 0) == r1, 1.0, 0.0).astype(BF16)
         by_row = by_row + dot_nt(hot_row, hot_key)
-        by_key = by_key + dot_nt(hot_key, jnp.concatenate([hot_row, jnp.zeros((112, 128), BF16)], axis=0))
-    key_ref[...] = by_key
-    for r in range(16):
-        row_ref[8 * r : 8 * r + 8, :] = jnp.broadcast_to(by_row[r : r + 1], (8, 128))
-
-
-def weigh(key_ref, row_ref, turned_ref, back_ref, acc_ref):
-    for r in range(16):
-        weighted = turned_ref[r] * jnp.broadcast_to(key_ref[:, r : r + 1], (128, 128))
-        for ka in range(4):
-            acc_ref[32 * r + 8 * ka : 32 * r + 8 * ka + 8, :] = jnp.sum(weighted[32 * ka : 32 * ka + 32].reshape(4, 8, 128), axis=0)
-
-    def step(i, carry):
-        for j in range(4):
-            r1 = 4 * i + j
-            counts = row_ref[rows(8 * r1, 8), :]
-            for kind, diff, slot in row_parts(i, j):
-                sums = {}
-                for ka, lo, hi in OWN_SPANS if kind == 4 else CROSS_SPANS:
-                    for kb in range(lo, hi + 1):
-                        key = key_of(kind, ka, kb)
-                        back = own_back(r1) if kind == 4 else cross_back(slot)
-                        b = back_ref[back(ka, kb)] * jnp.broadcast_to(counts[:, key : key + 1], (8, 128))
-                        sums[kb] = b if kb not in sums else sums[kb] + b
-                for kb, b in sums.items():
-                    acc_ref[rows((4 * (r1 + diff) + kb) * 8, 8), :] += b
-        return carry
-
-    lax.fori_loop(0, 3, step, 0)
-    step(3, 0)
-
-
-def far_field(got, u, v):
+    row_ref[...] = by_row
+
+
+def weigh_second(row_ref, high_ref, low_ref, first_ref):
+    row, lane = iota((16, 128), 0), iota((16, 128), 1)
+    mine = lane // 32 == row % 4
+    for g in range(8):
+        count = jnp.concatenate([jnp.broadcast_to(row_ref[2 * g + n : 2 * g + n + 1, :], (8, 128)) for n in (0, 1)], axis=0)
+        high = count.astype(BF16).astype(F32)
+        weight = jnp.where(mine, jnp.where(row % 8 < 4, high, count - high), 0.0).astype(BF16)
+        for n in (0, 1):
+            r = 2 * g + n
+            x = dot(weight, high_ref[r]) + dot(weight, low_ref[r])
+            first_ref[8 * r : 8 * r + 8, :] = x[8 * n : 8 * n + 8]
+
+
+def weigh_first(count_ref, back_ref, acc_ref):
+    sums = {}
+    for r1 in range(16):
+        for kind, diff, slot in row_parts(r1 // 4, r1 % 4):
+            for ka, lo, hi in OWN_SPANS if kind == 4 else CROSS_SPANS:
+                for kb in range(lo, hi + 1):
+                    back = own_back(r1) if kind == 4 else cross_back(slot)
+                    b = back_ref[back(ka, kb)] * count_ref[r1, key_of(kind, ka, kb)]
+                    box = 4 * (r1 + diff) + kb
+                    sums[box] = b if box not in sums else sums[box] + b
+    for box in range(64):
+        acc_ref[8 * box : 8 * box + 8, :] = sums.get(box, jnp.zeros((8, 128), F32))
+
+
+def far_geometry(u, v, far_ref):
     g, src = iota((64, 128), 0), iota((64, 128), 1)
     dx0 = (4 * (u - src % GX) + g // 16).astype(F32) + 0.5
     dy0 = (4 * (v - src // GX) + g // 4 % 4).astype(F32) + 0.5
     dz0 = (g % 4).astype(F32) + 0.5
-    total = jnp.zeros((64, 128), F32)
     for p in range(8):
         dx = dx0 - (2 * (p // 4) + 1)
         dy = dy0 - (2 * (p // 2 % 2) + 1)
         dz = dz0 - (2 * (p % 2) + 1)
-        total = total + lax.rsqrt(dx * dx + dy * dy + dz * dz + SOFT_TERM) * got[2 * CAP + p : 2 * CAP + 1 + p]
+        far_ref[p] = lax.rsqrt(dx * dx + dy * dy + dz * dz + SOFT_TERM)
+
+
+def far_field(got, distance_ref):
+    total = jnp.zeros((64, 128), F32)
+    for p in range(8):
+        total = total + distance_ref[p] * got[2 * CAP + p : 2 * CAP + 1 + p]
     col = jnp.sum(total, axis=1, keepdims=True)
     eye = iota((64, 64), 0) == iota((64, 64), 1)
     return jnp.sum(jnp.where(eye, col, 0.0), axis=0, keepdims=True)
 
 
-def collect(acc_ref, live, out_ref):
-    total = jnp.zeros((64, 128), F32)
-    for sub in range(8):
-        part = [acc_ref[pl.ds(64 * g + sub, 8, stride=8), :] for g in range(8)]
-        total = total + jnp.concatenate(part, axis=0)
-    out_ref[...] = jnp.where(live, total, 0.0)
+def collect(acc_ref, first_ref, live, out_ref):
+    total = []
+    for g in range(8):
+        x = [first_ref[16 * g + n : 16 * g + n + 4, :] + first_ref[16 * g + n + 4 : 16 * g + n + 8, :] for n in (0, 8)]
+        part = jnp.concatenate(x, axis=0)
+        for sub in range(8):
+            part = part + acc_ref[pl.ds(64 * g + sub, 8, stride=8), :]
+        total.append(part)
+    out_ref[...] = jnp.where(live, jnp.concatenate(total, axis=0), 0.0)
 
 
 def kernel(
     q_hbm, pos_hbm, wid_hbm, cnt_hbm, rec_hbm, near_ref, far_ref, q_ref, pos_ref, wid_ref, cnt_ref, rec_ref, in_sem,
-    left_ref, right_ref, lt_ref, rt_ref, ql_ref, qc_ref, set_ref, turned_ref, back_ref, key_ref, row_ref, acc_ref,
+    left_ref, right_ref, lt_ref, rt_ref, ql_ref, qc_ref, set_ref, high_ref, low_ref, back_ref, row_ref, count_ref, first_ref, distance_ref, acc_ref, count_sem,
     send_ref, mid_ref, turn_ref, got_ref, send1, recv1, send2, recv2,
 ):
     u, v = lax.axis_index("gx"), lax.axis_index("gy")
@@ -275,12 +284,12 @@
 
     wave = 40 * (v % 4) + 48 * (v // 4)
     enter = 100 + wave + 82 * (u // 2)
-    all_in = 100 + jnp.maximum(246 + wave, 264 + 82 * (u // 2)) + 150
-    crossed = 1110
+    all_in = 100 + jnp.maximum(246 + wave, 264 + 82 * (u // 2)) + 180
+    crossed = 1150
     ready = enter + 80
     late = all_in < ready + 100
-    pairs_first = jnp.where(late, 0, jnp.clip((all_in - ready - FEATURE_TIME + STEP_TIME // 2) // STEP_TIME, 0, STEPS))
-    pairs_second = jnp.clip((crossed - ready - FEATURE_TIME + STEP_TIME // 2) // STEP_TIME, pairs_first, STEPS)
+    pairs_first = jnp.where(late, 0, jnp.clip((all_in - ready - FEATURE_TIME) // STEP_TIME, 0, STEPS))
+    pairs_second = jnp.clip((crossed - ready - FEATURE_TIME) // STEP_TIME, pairs_first, STEPS)
 
     refs = (ql_ref, qc_ref, lt_ref, rt_ref, set_ref, back_ref)
 
@@ -341,15 +350,20 @@
     lax.fori_loop(pairs_second, STEPS, pair_step, 0)
     for r in (14, 15):
         produce_own(r, refs)
-    turn_sets(set_ref, turned_ref)
+    turn_sets(set_ref, high_ref, low_ref)
+    far_geometry(u, v, distance_ref)
 
     for copy in second:
         copy.wait_recv()
     got = got_ref[...].T
-    count_pairs(got, key_ref, row_ref)
-    far_ref[...] = far_field(got, u, v)
-    weigh(key_ref, row_ref, turned_ref, back_ref, acc_ref)
-    collect(acc_ref, live, near_ref)
+    count_pairs(got, row_ref)
+    counts = pltpu.make_async_copy(row_ref, count_ref, count_sem)
+    counts.start()
+    weigh_second(row_ref, high_ref, low_ref, first_ref)
+    far_ref[...] = far_field(got, distance_ref)
+    counts.wait()
+    weigh_first(count_ref, back_ref, acc_ref)
+    collect(acc_ref, first_ref, live, near_ref)
     for copy in first + second:
         copy.wait_send()
 
@@ -375,11 +389,15 @@
             vmem((64, 128), F32),
             vmem((8192, 128), F32),
             vmem((PAIRS + 16, 128, 128), F32),
-            vmem((16, 128, 128), F32),
+            vmem((16, 128, 128), BF16),
+            vmem((16, 128, 128), BF16),
             vmem((468, 8, 128), F32),
+            vmem((16, 128), F32),
+            pltpu.SMEM((16, 128), F32),
             vmem((128, 128), F32),
-            vmem((128, 128), F32),
+            vmem((8, 64, 128), F32),
             vmem((512, 128), F32),
+            pltpu.SemaphoreType.DMA,
             vmem((DEVICES, 128), F32),
             vmem((DEVICES, 128), F32),
             vmem((DEVICES, 128), F32),

time: 21.3 us -> 20.7 us (0.972)
  Pallas kernels: 19.4 us -> 18.8 us
    pallas_call x1, Pallas kernels: 19.4 us -> 18.8 us  [body(): pl.pallas_call(kernel, out_shape=(vmem((64, 128), F32), vmem((1, 64), F32...]
where the time goes in v5:
time: 20.7 us; the launch traced here: 20.6 us
  Pallas kernels  18.8 us (91%)
  local copies, waits for them, and re-layouts  1.13 us (5%)
  between operations  0.64 us (3%)
    pallas_call x1, Pallas kernels, body(): pl.pallas_call(kernel, out_shape=(vmem((64, 128), F32), vmem((1, 64), F32...  18.8 us
    unnamed x2, local copies, waits for them, and re-layouts  1.13 us

profile of v5, /device:TPU:1, one launch (start us, length us, event | category | flops | bytes accessed | tf_op | source)
XLA Modules:
  0.0 20.6 jit_solution(16457190700337611682)
XLA Ops:
  0.6 18.8 %shard_map.68 = (f32[64,128]{1,0:T(8,128)S(1)}, f32[1,64]{1,0:T(1,128)S(1)}) custom-call(f32[64,128]{1,0:T(8,128)} %q_hbm.1, f32[3,64,128]{2,1,0:T(8,128)} %bitcast.5, f32[64,128]{1,0:T(8,128)} %wid_hbm.1, s32[1,64]{1,0:T(1,128)} %bitcast.7, s32[3,256]{1,0:T(4,128)} %bitcast.6), custom_call_target="tpu_custom_call" | custom-call | tf_op jit(solution)/shard_map/pallas_call | solution.py:373
  19.5 0.6 %copy.9 = f32[64,128]{1,0:T(8,128)} copy(f32[64,128]{1,0:T(8,128)S(1)} %get-tuple-element.6) | data formatting | bytes 65536
  20.1 0.5 %copy.10 = f32[64]{0:T(128)} copy(f32[64]{0:T(128)S(1)} %bitcast.4) | data formatting | bytes 512

commit v6 on v5

--- a/solution.py
+++ b/solution.py
@@ -8,10 +8,11 @@
 F32, BF16, I32 = jnp.float32, jnp.bfloat16, jnp.int32
 MESH = pl.DeviceIdType.MESH
 GX, GY, CAP = 8, 16, 8
+HEADS, HEAD_STEPS = 2, 6
 DEVICES = GX * GY
 DEPTH = 48
 SOFT_TERM = 2.0
-FEATURE_TIME, STEP_TIME = 150, 136
+FEATURE_TIME, STEP_TIME = 140, 70
 
 
 def iota(shape, dim):
@@ -101,8 +102,7 @@
 CROSS_SPANS = [(ka, *span(ka)) for ka in range(4)]
 OWN_SPANS = [(ka, ka + 1, ka + 1) for ka in range(3)]
 PAIRS = 42
-TRIPLES = 2
-STEPS = 14 // TRIPLES
+STEPS = 14
 
 
 def key_of(kind, ka, kb):
@@ -143,13 +143,26 @@
     produce(r, r, 4, PAIRS + r, OWN_SPANS, own_back(r), *refs)
 
 
-def produce_step(step, refs):
-    for n in range(TRIPLES):
-        t = TRIPLES * step + n
-        base, diff, kind = step_rows(t)
-        for j in range(3):
-            produce(base + j, base + j + diff, kind, 3 * t + j, CROSS_SPANS, cross_back(3 * t + j), *refs)
-        produce_own(t, refs)
+def produce_triple(t, refs):
+    base, diff, kind = step_rows(t)
+    for j in range(3):
+        produce(base + j, base + j + diff, kind, 3 * t + j, CROSS_SPANS, cross_back(3 * t + j), *refs)
+    produce_own(t, refs)
+
+
+def produce_range(start, stop, refs):
+    def one(t, carry):
+        produce_triple(t, refs)
+        return carry
+
+    def two(t, carry):
+        produce_triple(2 * t, refs)
+        produce_triple(2 * t + 1, refs)
+        return carry
+
+    lax.fori_loop(start, jnp.minimum(stop, start + start % 2), one, 0)
+    lax.fori_loop((start + 1) // 2, stop // 2, two, 0)
+    lax.fori_loop(jnp.maximum(stop - stop % 2, start + start % 2), stop, one, 0)
 
 
 def row_parts(i, j):
@@ -185,17 +198,16 @@
 
 
 def count_pairs(got, row_ref):
-    by_row = jnp.zeros((16, 128), F32)
+    hot_row, hot_key = [], []
     for k in range(CAP):
         a, b = got[k : k + 1].astype(I32) - 1, got[CAP + k : CAP + 1 + k].astype(I32) - 1
         first, second = jnp.minimum(a, b), jnp.maximum(a, b)
         r1, diff = first // 4, second // 4 - first // 4
         kind = jnp.where(diff == 0, 4, jnp.where(diff == 1, 0, jnp.where(diff == 3, 1, jnp.where(diff == 5, 2, 3))))
         key = jnp.where(first >= 0, 32 * (first % 4) + 4 * kind + second % 4, 128)
-        hot_key = jnp.where(iota((128, 128), 0) == key, 1.0, 0.0).astype(BF16)
-        hot_row = jnp.where(iota((16, 128), 0) == r1, 1.0, 0.0).astype(BF16)
-        by_row = by_row + dot_nt(hot_row, hot_key)
-    row_ref[...] = by_row
+        hot_key.append(jnp.where(iota((128, 128), 0) == key, 1.0, 0.0).astype(BF16))
+        hot_row.append(jnp.where(iota((16, 128), 0) == r1, 1.0, 0.0).astype(BF16))
+    row_ref[...] = dot_nt(jnp.concatenate(hot_row, axis=1), jnp.concatenate(hot_key, axis=1))
 
 
 def weigh_second(row_ref, high_ref, low_ref, first_ref):
@@ -260,7 +272,7 @@
 def kernel(
     q_hbm, pos_hbm, wid_hbm, cnt_hbm, rec_hbm, near_ref, far_ref, q_ref, pos_ref, wid_ref, cnt_ref, rec_ref, in_sem,
     left_ref, right_ref, lt_ref, rt_ref, ql_ref, qc_ref, set_ref, high_ref, low_ref, back_ref, row_ref, count_ref, first_ref, distance_ref, acc_ref, count_sem,
-    send_ref, mid_ref, turn_ref, got_ref, send1, recv1, send2, recv2,
+    send_ref, mid_ref, turn_ref, got_ref, send1, recv1, send2, recv2, head_ref, heard_ref, send3, recv3,
 ):
     u, v = lax.axis_index("gx"), lax.axis_index("gy")
     pairs = ((rec_hbm, rec_ref), (cnt_hbm, cnt_ref), (q_hbm, q_ref), (pos_hbm, pos_ref), (wid_hbm, wid_ref))
@@ -270,11 +282,21 @@
     others_x = [lax.rem(u + s, GX) for s in range(1, GX)]
     others_y = [lax.rem(v + s, GY) for s in range(1, GY)]
     barrier = pltpu.get_barrier_semaphore()
+    is_head = (u < HEADS) & (v == 0)
+    far_heads = [(u != e) & (v != 0) for e in range(HEADS)]
+    for y in others_y:
+        pl.semaphore_signal(barrier, inc=1, device_id=(u, y), device_id_type=MESH)
     for x in others_x:
         pl.semaphore_signal(barrier, inc=1, device_id=(x, v), device_id_type=MESH)
-    for y in others_y:
-        pl.semaphore_signal(barrier, inc=1, device_id=(u, y), device_id_type=MESH)
-
+
+
+    def greet_all():
+        for x in others_x:
+            for y in others_y:
+                pl.semaphore_signal(barrier, inc=1, device_id=(x, y), device_id_type=MESH)
+
+    pl.when(is_head)(greet_all)
+    far_geometry(u, v, distance_ref)
     for copy in inputs[:3]:
         copy.wait()
     cnt = column(cnt_ref[...].astype(F32)).astype(I32)
@@ -283,19 +305,16 @@
     messages(rec_ref, ql_ref, send_ref)
 
     wave = 40 * (v % 4) + 48 * (v // 4)
-    enter = 100 + wave + 82 * (u // 2)
-    all_in = 100 + jnp.maximum(246 + wave, 264 + 82 * (u // 2)) + 180
-    crossed = 1150
+    enter = 100 + wave + 82 * (u // 2) - jnp.where((u == 1) & (v == 0), 80, 0)
+    all_in = 100 + jnp.maximum(246 + wave, 264 + 82 * (u // 2)) + 185
+    crossed = 1110
     ready = enter + 80
     late = all_in < ready + 100
     pairs_first = jnp.where(late, 0, jnp.clip((all_in - ready - FEATURE_TIME) // STEP_TIME, 0, STEPS))
+    pairs_first = jnp.where(is_head, HEAD_STEPS, pairs_first)
     pairs_second = jnp.clip((crossed - ready - FEATURE_TIME) // STEP_TIME, pairs_first, STEPS)
 
     refs = (ql_ref, qc_ref, lt_ref, rt_ref, set_ref, back_ref)
-
-    def pair_step(t, carry):
-        produce_step(t, refs)
-        return carry
 
     def make_features():
         for g in range(8):
@@ -313,25 +332,34 @@
         for s, x in enumerate(others_x)
     ]
 
+    to_heads = [
+        pltpu.make_async_remote_copy(
+            src_ref=head_ref.at[e],
+            dst_ref=heard_ref.at[v * GX + u],
+            send_sem=send3.at[e],
+            recv_sem=recv3,
+            device_id=(e, 0),
+            device_id_type=MESH,
+        )
+        for e in range(HEADS)
+    ]
+    not_head = [jnp.logical_not((u == e) & (v == 0)) for e in range(HEADS)]
+
     def send_first():
-        pl.semaphore_wait(barrier, GX + GY - 2)
+        pl.semaphore_wait(barrier, GX + GY - 2 + sum(x.astype(I32) for x in far_heads))
         for copy in first:
             copy.start()
+        for e in range(HEADS):
+            pl.when(not_head[e])(to_heads[e].start)
 
     for copy in inputs[3:]:
         copy.wait()
     planes(pos_ref, wid_ref, left_ref, right_ref)
     mid_ref[rows(u * GY, GY), :] = send_ref[rows(u * GY, GY), :]
+    for e in range(HEADS):
+        head_ref[e] = send_ref[GY * e : GY * e + 1, :]
     pl.when(late)(send_first)
     make_features()
-    lax.fori_loop(0, pairs_first, pair_step, 0)
-    pl.when(jnp.logical_not(late))(send_first)
-    lax.fori_loop(pairs_first, pairs_second, pair_step, 0)
-
-    for copy in first:
-        copy.wait_recv()
-    for y in range(GY):
-        turn_ref[y * GX : (y + 1) * GX, :] = mid_ref[pl.ds(y, GX, stride=GY), :]
     second = [
         pltpu.make_async_remote_copy(
             src_ref=turn_ref.at[rows(y * GX, GX)],
@@ -343,18 +371,45 @@
         )
         for s, y in enumerate(others_y)
     ]
-    for copy in second:
-        copy.start()
-    got_ref[rows(v * GX, GX), :] = turn_ref[rows(v * GX, GX), :]
-
-    lax.fori_loop(pairs_second, STEPS, pair_step, 0)
+    into_head = [(u < HEADS) & (y == 0) for y in others_y]
+
+    def pass_on():
+        for copy in first:
+            copy.wait_recv()
+        for y in range(GY):
+            turn_ref[y * GX : (y + 1) * GX, :] = mid_ref[pl.ds(y, GX, stride=GY), :]
+        for copy, skip in zip(second, into_head):
+            pl.when(jnp.logical_not(skip))(copy.start)
+        pl.when(jnp.logical_not(is_head))(keep_own)
+
+    def keep_own():
+        got_ref[rows(v * GX, GX), :] = turn_ref[rows(v * GX, GX), :]
+
+    def part(n, carry):
+        start = jnp.where(n == 0, 0, jnp.where(n == 1, pairs_first, pairs_second))
+        stop = jnp.where(n == 0, pairs_first, jnp.where(n == 1, pairs_second, STEPS))
+        produce_range(start, stop, refs)
+        pl.when((n == 0) & jnp.logical_not(late))(send_first)
+        pl.when(n == 1)(pass_on)
+        return carry
+
+    lax.fori_loop(0, 3, part, 0)
     for r in (14, 15):
         produce_own(r, refs)
     turn_sets(set_ref, high_ref, low_ref)
-    far_geometry(u, v, distance_ref)
-
-    for copy in second:
-        copy.wait_recv()
+
+    def hear():
+        pltpu.make_async_copy(heard_ref.at[pl.ds(0, DEVICES - 1)], heard_ref.at[pl.ds(0, DEVICES - 1)], recv3).wait()
+        own = send_ref[rows(u * GY, 8), :][0:1]
+        source = iota((DEVICES, 128), 0)
+        got_ref[...] = jnp.where(source == v * GX + u, own, heard_ref[:, 0, :])
+
+    def take():
+        for copy in second:
+            copy.wait_recv()
+
+    pl.when(is_head)(hear)
+    pl.when(jnp.logical_not(is_head))(take)
     got = got_ref[...].T
     count_pairs(got, row_ref)
     counts = pltpu.make_async_copy(row_ref, count_ref, count_sem)
@@ -364,8 +419,12 @@
     counts.wait()
     weigh_first(count_ref, back_ref, acc_ref)
     collect(acc_ref, first_ref, live, near_ref)
-    for copy in first + second:
+    for copy in first:
         copy.wait_send()
+    for copy, skip in zip(second, into_head):
+        pl.when(jnp.logical_not(skip))(copy.wait_send)
+    for e in range(HEADS):
+        pl.when(not_head[e])(to_heads[e].wait_send)
 
 
 def body(charges, positions, widths, site_counts, pair_records):
@@ -406,6 +465,10 @@
             pltpu.SemaphoreType.DMA((GX - 1,)),
             pltpu.SemaphoreType.DMA((GY - 1,)),
             pltpu.SemaphoreType.DMA((GY - 1,)),
+            vmem((HEADS, 1, 128), F32),
+            vmem((DEVICES, 1, 128), F32),
+            pltpu.SemaphoreType.DMA((HEADS,)),
+            pltpu.SemaphoreType.DMA,
         ],
         compiler_params=pltpu.CompilerParams(collective_id=0, has_side_effects=True, vmem_limit_bytes=56 << 20),
     )(charges, positions.transpose(1, 0, 2), widths, site_counts.reshape(1, 64), pair_records.T)

time: 20.7 us -> 19.9 us (0.961)
  the two profiles are of different devices: /device:TPU:1 before, /device:TPU:32 now
where the time goes in v6:
time: 19.9 us; the launch traced here: 19.8 us
  Pallas kernels  18 us (90%)
  local copies, waits for them, and re-layouts  1.13 us (6%)
  between operations  0.64 us (3%)
    pallas_call x1, Pallas kernels, body(): pl.pallas_call(kernel, out_shape=(vmem((64, 128), F32), vmem((1, 64), F32...  18 us
    unnamed x2, local copies, waits for them, and re-layouts  1.13 us

profile of v6, /device:TPU:32, one launch (start us, length us, event | category | flops | bytes accessed | tf_op | source)
XLA Modules:
  0.0 19.8 jit_solution(7584317503856599211)
XLA Ops:
  0.6 18.0 %shard_map.68 = (f32[64,128]{1,0:T(8,128)S(1)}, f32[1,64]{1,0:T(1,128)S(1)}) custom-call(f32[64,128]{1,0:T(8,128)} %q_hbm.1, f32[3,64,128]{2,1,0:T(8,128)} %bitcast.5, f32[64,128]{1,0:T(8,128)} %wid_hbm.1, s32[1,64]{1,0:T(1,128)} %bitcast.7, s32[3,256]{1,0:T(4,128)} %bitcast.6), custom_call_target="tpu_custom_call" | custom-call | tf_op jit(solution)/shard_map/pallas_call | solution.py:432
  18.7 0.6 %copy.9 = f32[64,128]{1,0:T(8,128)} copy(f32[64,128]{1,0:T(8,128)S(1)} %get-tuple-element.6) | data formatting | bytes 65536
  19.3 0.5 %copy.10 = f32[64]{0:T(128)} copy(f32[64]{0:T(128)S(1)} %bitcast.4) | data formatting | bytes 512

commit v7 on v6

--- a/solution.py
+++ b/solution.py
@@ -155,14 +155,15 @@
         produce_triple(t, refs)
         return carry
 
-    def two(t, carry):
-        produce_triple(2 * t, refs)
-        produce_triple(2 * t + 1, refs)
+    def three(t, carry):
+        for n in range(3):
+            produce_triple(3 * t + n, refs)
         return carry
 
-    lax.fori_loop(start, jnp.minimum(stop, start + start % 2), one, 0)
-    lax.fori_loop((start + 1) // 2, stop // 2, two, 0)
-    lax.fori_loop(jnp.maximum(stop - stop % 2, start + start % 2), stop, one, 0)
+    begin, end = (start + 2) // 3, stop // 3
+    lax.fori_loop(start, jnp.minimum(stop, 3 * begin), one, 0)
+    lax.fori_loop(begin, end, three, 0)
+    lax.fori_loop(jnp.maximum(3 * end, 3 * begin), stop, one, 0)
 
 
 def row_parts(i, j):

time: 19.9 us -> 19.9 us (level)
  no operation moved by 1% of the time
where the time goes in v7:
time: 19.9 us; the launch traced here: 19.8 us
  Pallas kernels  18 us (90%)
  local copies, waits for them, and re-layouts  1.13 us (6%)
  between operations  0.64 us (3%)
    pallas_call x1, Pallas kernels, body(): pl.pallas_call(kernel, out_shape=(vmem((64, 128), F32), vmem((1, 64), F32...  18 us
    unnamed x2, local copies, waits for them, and re-layouts  1.13 us

profile of v7, /device:TPU:32, one launch (start us, length us, event | category | flops | bytes accessed | tf_op | source)
XLA Modules:
  0.0 19.8 jit_solution(14731902868085635289)
XLA Ops:
  0.6 18.0 %shard_map.68 = (f32[64,128]{1,0:T(8,128)S(1)}, f32[1,64]{1,0:T(1,128)S(1)}) custom-call(f32[64,128]{1,0:T(8,128)} %q_hbm.1, f32[3,64,128]{2,1,0:T(8,128)} %bitcast.5, f32[64,128]{1,0:T(8,128)} %wid_hbm.1, s32[1,64]{1,0:T(1,128)} %bitcast.7, s32[3,256]{1,0:T(4,128)} %bitcast.6), custom_call_target="tpu_custom_call" | custom-call | tf_op jit(solution)/shard_map/pallas_call | solution.py:433
  18.6 0.6 %copy.9 = f32[64,128]{1,0:T(8,128)} copy(f32[64,128]{1,0:T(8,128)S(1)} %get-tuple-element.6) | data formatting | bytes 65536
  19.3 0.5 %copy.10 = f32[64]{0:T(128)} copy(f32[64]{0:T(128)S(1)} %bitcast.4) | data formatting | bytes 512
